TPU v7x, 256 devices: a whole 4x4x8 slice. The times are simulated.
256 devices in a mesh: xy: 64 (over x, y, z_lo, core), gz: 4 (over z_hi).
Axes of the slice: x: 4, y: 4, z: 8 (z_hi: 4, z_lo: 2; z = z_hi * 2 + z_lo), core: 2. Of those that a mesh axis runs over, the one named last changes fastest.
Arguments:
- electric: float32 [4, 2048, 2048], P('gz', 'xy'), may hold values from -6 to 6
- magnetic_first: float32 [4, 2048, 2048], P('gz', 'xy'), may hold values from -6 to 6
- magnetic_second: float32 [4, 2048, 2048], P('gz', 'xy'), may hold values from -6 to 6
- region: int32 [4, 2048, 2048], P('gz', 'xy'), may hold values from 0 to 7
- permittivity_table: float32 [8], replicated, may hold values from 1 to 12
- conductivity_table: float32 [8], replicated, may hold values from 0.02 to 4
Outputs:
- electric_final: float32 [4, 2048, 2048], P('gz', 'xy')
- first_final: float32 [4, 2048, 2048], P('gz', 'xy')
- second_final: float32 [4, 2048, 2048], P('gz', 'xy')
All inputs are finite; a program needn't handle non-finite values.
Results may differ from a plain program's by a relative error of at most 0.000024.
Values sent between devices are 32-bit elements; how exact they have to be, the bound alone decides.
No kernel may reach another device: no remote copies, remote signals or barrier semaphores. Data moves between devices by JAX's collectives and lax.ppermute only.
A program may use at most 64 MiB of HBM per device.

v0:
```python
import jax
import jax.numpy as jnp
from jax import lax
from jax.experimental import pallas as pl
from jax.experimental.pallas import tpu as pltpu
from jax.sharding import PartitionSpec as P

RATE = 4.0
KAPPA = 0.5
ROWS = 32
LINE = 2048
PEERS = 64
TILES = LINE // 128
F32 = jnp.float32
LEVELS = 11
SEGMENT = 8
GROUPS = 8
CUT_LEVELS = 8


def index(shape, axis):
    return lax.broadcasted_iota(jnp.int32, shape, axis)


def swap_blocks(tiles, lane):
    left = lane < 64
    even = (lane & 32) == 0
    half = [None] * 4
    for low in range(2):
        a, b = tiles[low], tiles[low + 2]
        half[low] = jnp.where(left, a, pltpu.roll(b, 64, 1))
        half[low + 2] = jnp.where(left, pltpu.roll(a, 64, 1), b)
    out = [None] * 4
    for high in (0, 2):
        a, b = half[high], half[high + 1]
        out[high] = jnp.where(even, a, pltpu.roll(b, 32, 1))
        out[high + 1] = jnp.where(even, pltpu.roll(a, 96, 1), b)
    return out


def pack(source, target, first):
    lane = index((8, 128), 1)
    for q in range(TILES):
        tiles = [source[8 * u : 8 * u + 8, 128 * q : 128 * q + 128] for u in range(4)]
        for b, tile in enumerate(swap_blocks(tiles, lane)):
            target[4 * q + b, first : first + 8, :] = tile


def turned(tile_of, lane):
    for wide in range(4):
        columns = []
        for s in range(4):
            columns += swap_blocks([tile_of(16 * wide + 4 * g + s) for g in range(4)], lane)
        square = jnp.concatenate(columns, axis=0).T
        for g in range(4):
            yield 128 * (4 * wide + g), square[32 * g : 32 * g + 32, :]


def from_before(values, step, lane):
    if step >= 128:
        jump = step // 128
        return [None] * jump + values[: TILES - jump]
    moved = [pltpu.roll(v, step, 1) for v in values]
    edge = lane < step
    return [jnp.where(edge, moved[k - 1] if k else 0.0, moved[k]) for k in range(TILES)]


def from_after(values, step, lane, wrap=False):
    if step >= 128:
        jump = step // 128
        return values[jump:] + [None] * jump
    moved = [pltpu.roll(v, 128 - step, 1) for v in values]
    edge = lane >= 128 - step
    moved.append(moved[0] if wrap else 0.0)
    return [jnp.where(edge, moved[k + 1], moved[k]) for k in range(TILES)]


def cut_before(values, step):
    if step >= 32:
        jump = step // 32
        return [None] * jump + values[: GROUPS - jump]
    row, lane = index((8, 128), 0), index((8, 128), 1)
    if step >= 4:
        count = step // 4
        moved = [pltpu.roll(v, count, 0) for v in values]
        edge = row < count
        return [jnp.where(edge, moved[k - 1] if k else 0.0, moved[k]) for k in range(GROUPS)]
    aside = [pltpu.roll(v, 32 * step, 1) for v in values]
    moved = [pltpu.roll(v, 1, 0) for v in aside]
    edge = row < 1
    return [
        jnp.where(
            lane < 32 * step,
            jnp.where(edge, moved[k - 1] if k else 0.0, moved[k]),
            aside[k],
        )
        for k in range(GROUPS)
    ]


def cut_after(values, step, wrap=False):
    if step >= 32:
        jump = step // 32
        return values[jump:] + [None] * jump
    row, lane = index((8, 128), 0), index((8, 128), 1)
    if step >= 4:
        count = step // 4
        moved = [pltpu.roll(v, 8 - count, 0) for v in values] + [0.0]
        edge = row >= 8 - count
        return [jnp.where(edge, moved[k + 1], moved[k]) for k in range(GROUPS)]
    aside = [pltpu.roll(v, 128 - 32 * step, 1) for v in values]
    moved = [pltpu.roll(v, 7, 0) for v in aside]
    moved.append(moved[0] if wrap else 0.0)
    edge = row >= 7
    return [
        jnp.where(
            lane >= 128 - 32 * step, jnp.where(edge, moved[k + 1], moved[k]), aside[k]
        )
        for k in range(GROUPS)
    ]


def minus(a, b):
    return a if b is None else a - b


def times(a, b):
    return None if a is None or b is None else a * b


def read(ref):
    return [ref[:, 128 * k : 128 * k + 128] for k in range(TILES)]


def write(ref, values):
    for k, v in enumerate(values):
        ref[:, 128 * k : 128 * k + 128] = v


def factor_level(diagonal, couple, step, before, after):
    weight = [1.0 / d for d in diagonal]
    pull = [times(w, c) for w, c in zip(weight, couple)]
    low = [times(c, w) for c, w in zip(couple, before(weight, step))]
    high = after(pull, step)
    loss = after([times(c, g) for c, g in zip(couple, pull)], step)
    diagonal = [
        minus(minus(d, times(c, a)), b) for d, c, a, b in zip(diagonal, couple, low, loss)
    ]
    couple = [times(a, c) for a, c in zip(low, before(couple, step))]
    return diagonal, couple, low, high


def reduce_level(right, low, high, step, before, after):
    out = []
    for r, a, b, x, y in zip(right, low, high, before(right, step), after(right, step)):
        if x is not None:
            r = r + a * x
        if y is not None:
            r = r + b * y
        out.append(r)
    return out


def factor_lines(diagonal, lane, coef_ref):
    def store(at, values):
        for k, v in enumerate(values):
            if v is not None:
                coef_ref[at, :, 128 * k : 128 * k + 128] = v

    def before(values, step):
        return from_before(values, step, lane)

    def after(values, step):
        return from_after(values, step, lane)

    square = RATE * RATE
    weight = [1.0 / d for d in diagonal]
    left, right = before(weight, 1), after(weight, 1)
    store(0, [RATE * w for w in left])
    store(1, [RATE * w for w in right])
    diagonal = [d - square * (a + b) for d, a, b in zip(diagonal, left, right)]
    couple = [square * w for w in left]
    couple[0] = jnp.where(lane >= 2, couple[0], 0.0)
    for level in range(1, LEVELS):
        diagonal, couple, low, high = factor_level(diagonal, couple, 1 << level, before, after)
        store(2 * level, low)
        store(2 * level + 1, high)
    store(2 * LEVELS, [1.0 / d for d in diagonal])


def reduce_lines(right, lane, coef_ref):
    def load(at):
        return [coef_ref[at, :, 128 * k : 128 * k + 128] for k in range(TILES)]

    def before(values, step):
        return from_before(values, step, lane)

    def after(values, step):
        return from_after(values, step, lane)

    for level in range(LEVELS):
        right = reduce_level(right, load(2 * level), load(2 * level + 1), 1 << level, before, after)
    return [r * w for r, w in zip(right, load(2 * LEVELS))]


def rows_kernel(e_ref, hx_ref, below_ref, e_scr, hx_scr, sem):
    tail = pl.ds(ROWS - 8, 8)
    copies = [
        pltpu.make_async_copy(hx_ref.at[tail], hx_scr, sem.at[0]),
        pltpu.make_async_copy(e_ref.at[tail], e_scr, sem.at[1]),
    ]
    for c in copies:
        c.start()
    for c in copies:
        c.wait()
    below_ref[0:1, :] = hx_scr[7:8, :]
    below_ref[1:2, :] = e_scr[7:8, :]


def send_kernel(
    region_hbm, e_hbm, hx_hbm, eps_ref, sig_ref, below_ref,
    early_ref, dplus_ref, dminus_ref, e_ref, hx_ref,
    region_ref, shifted_ref, sem,
):
    copies = [
        pltpu.make_async_copy(region_hbm, region_ref, sem.at[0]),
        pltpu.make_async_copy(e_hbm, e_ref, sem.at[1]),
        pltpu.make_async_copy(hx_hbm, hx_ref, sem.at[2]),
    ]
    for c in copies:
        c.start()
    plus_table = []
    minus_table = []
    for entry in range(8):
        eps = eps_ref[entry] / RATE
        sig = 0.5 * sig_ref[entry]
        plus_table.append(eps + sig)
        minus_table.append(eps - sig)
    row = index((ROWS, 128), 0)
    inside = lax.axis_index("xy") > 0
    for c in copies:
        c.wait()
    for k, here in enumerate(read(region_ref)):
        at = pl.ds(128 * k, 128)
        a = jnp.full((ROWS, 128), plus_table[0])
        b = jnp.full((ROWS, 128), minus_table[0])
        for entry in range(1, 8):
            mask = here == entry
            a = jnp.where(mask, plus_table[entry], a)
            b = jnp.where(mask, minus_table[entry], b)
        dplus_ref[:, at] = a
        dminus_ref[:, at] = b
        e = e_ref[:, at]
        edge = below_ref[0:1, at] - RATE * (jnp.where(inside, e[0:1], 0.0) - below_ref[1:2, at])
        half_hx = hx_ref[:, at] - RATE * (pltpu.roll(e, ROWS - 1, 0) - e)
        shifted_ref[:, at] = jnp.where(row == 0, edge, pltpu.roll(half_hx, 1, 0))
    pack(dplus_ref, early_ref, 0)
    pack(shifted_ref, early_ref, 8)


def start_kernel(
    dplus_ref, dminus_ref, e_ref, hx_ref, hy_hbm, below_ref, coef_ref, base_ref, hy_ref, sem
):
    copy = pltpu.make_async_copy(hy_hbm, hy_ref, sem)
    copy.start()
    lane = index((ROWS, 128), 1)
    row = index((ROWS, 128), 0)
    diagonal = [
        d + (2.0 * RATE if k else jnp.where(lane > 0, 2.0 * RATE, RATE))
        for k, d in enumerate(read(dplus_ref))
    ]
    factor_lines(diagonal, lane, coef_ref)
    inside = lax.axis_index("xy") > 0
    copy.wait()
    hy_before = from_before(read(hy_ref), 1, lane)
    for k in range(TILES):
        at = pl.ds(128 * k, 128)
        hx = hx_ref[:, at]
        edge = jnp.where(inside, below_ref[0:1, at], 0.0)
        hx_before = jnp.where(row == 0, edge, pltpu.roll(hx, 1, 0))
        e = e_ref[:, at]
        base_ref[:, at] = (
            dminus_ref[:, at] * e + (hy_ref[:, at] - hy_before[k]) - (hx - hx_before) - (2.0 * KAPPA) * e
        )


def first_kernel(base_ref, up_ref, down_ref, coef_ref, half_ref, packed_ref):
    lane = index((ROWS, 128), 1)
    right = [
        b + KAPPA * (u + d) for b, u, d in zip(read(base_ref), read(up_ref), read(down_ref))
    ]
    write(half_ref, reduce_lines(right, lane, coef_ref))
    pack(half_ref, packed_ref, 0)


def between_kernel(half_ref, dminus_ref, hy_ref, base_ref, full_hy_ref, b_scr, h_scr):
    lane = index((ROWS, 128), 1)
    half = read(half_ref)
    change = [RATE * (a - h) for a, h in zip(from_after(half, 1, lane), half)]
    half_hy = [a + b for a, b in zip(read(hy_ref), change)]
    write(h_scr, [a + b for a, b in zip(half_hy, change)])
    hy_before = from_before(half_hy, 1, lane)
    for k, (m, h) in enumerate(zip(read(dminus_ref), half)):
        b_scr[:, 128 * k : 128 * k + 128] = m * h + (half_hy[k] - hy_before[k]) - (2.0 * KAPPA) * h
    pack(h_scr, full_hy_ref, 0)
    pack(b_scr, base_ref, 0)


def merge_kernel(hy_ref, base_ref, up_ref, down_ref, late_ref):
    late_ref[:, 0:8, :] = base_ref[...] + KAPPA * (up_ref[...] + down_ref[...])
    late_ref[:, 8:16, :] = hy_ref[...]


def lines_kernel(early_ref, forth_ref, back_ref, cut_ref, drop_ref, hx_ref):
    lane = index((8, 128), 1)
    row = index((8, 128), 0)

    def tiles(which):
        return lambda s: early_ref[16 * s + 8 * which : 16 * s + 8 * which + 8, :]

    def cells(which, v):
        return [early_ref[pl.ds(128 * g + 8 * which + v, 8, stride=16), :] for g in range(GROUPS)]

    blocks = [block for _, block in turned(tiles(1), lane)]
    write(hx_ref, from_after(blocks, 1, index((ROWS, 128), 1), wrap=True))

    def put(ref, at, values):
        for g, value in enumerate(values):
            if value is not None:
                ref[at, 8 * g : 8 * g + 8, :] = value

    first_segment = (row == 0) & (lane < 32)
    shifted = [cells(1, v) for v in range(SEGMENT)]
    after = cut_after(shifted[0], 1, wrap=True)
    shifted.append(after)
    for v in range(SEGMENT):
        before = list(shifted[v])
        if v == 0:
            before[0] = jnp.where(first_segment, 0.0, before[0])
        put(drop_ref, v, [a - b for a, b in zip(shifted[v + 1], before)])

    diagonal = [[d + 2.0 * RATE for d in cells(0, v)] for v in range(SEGMENT)]
    diagonal[0][0] = diagonal[0][0] - jnp.where(first_segment, RATE, 0.0)
    inner = SEGMENT - 1
    forth = [RATE / d for d in diagonal[0]]
    put(forth_ref, 0, forth)
    product = forth
    for v in range(1, inner):
        forth = [RATE / (d - RATE * p) for d, p in zip(diagonal[v], forth)]
        put(forth_ref, v, forth)
        product = [a * b for a, b in zip(product, forth)]
    back = [RATE / d for d in diagonal[inner - 1]]
    put(back_ref, inner - 1, back)
    for v in range(inner - 2, -1, -1):
        back = [RATE / (d - RATE * p) for d, p in zip(diagonal[v], back)]
        put(back_ref, v, back)
    couple = [RATE * p for p in product]
    couple[0] = jnp.where(first_segment, 0.0, couple[0])
    diagonal = [
        d - RATE * (a + b) for d, a, b in zip(diagonal[inner], forth, cut_after(back, 1))
    ]
    for level in range(CUT_LEVELS):
        diagonal, couple, low, high = factor_level(
            diagonal, couple, 1 << level, cut_before, cut_after
        )
        put(cut_ref, 2 * level, low)
        put(cut_ref, 2 * level + 1, high)
    put(cut_ref, 2 * CUT_LEVELS, [1.0 / d for d in diagonal])


def second_kernel(
    late_ref, forth_ref, back_ref, cut_ref, drop_ref, half_hx_ref, e_ref, hx_ref, hy_ref, full_scr
):
    def get(ref, at):
        return [ref[at, 8 * g : 8 * g + 8, :] for g in range(GROUPS)]

    inner = SEGMENT - 1
    right = [
        [
            late_ref[pl.ds(128 * g + v, 8, stride=16), :] - d
            for g, d in enumerate(get(drop_ref, v))
        ]
        for v in range(SEGMENT)
    ]
    forth = [p * r for p, r in zip(get(forth_ref, 0), right[0])]
    back = [p * r for p, r in zip(get(back_ref, inner - 1), right[inner - 1])]
    for v in range(1, inner):
        forth = [p * (r + u) for p, r, u in zip(get(forth_ref, v), right[v], forth)]
        w = inner - 1 - v
        back = [p * (r + u) for p, r, u in zip(get(back_ref, w), right[w], back)]
    between = [r + a + b for r, a, b in zip(right[inner], forth, cut_after(back, 1))]
    for level in range(CUT_LEVELS):
        between = reduce_level(
            between, get(cut_ref, 2 * level), get(cut_ref, 2 * level + 1), 1 << level, cut_before, cut_after
        )
    between = [r * w for r, w in zip(between, get(cut_ref, 2 * CUT_LEVELS))]

    def put(v, values):
        for g, value in enumerate(values):
            full_scr[pl.ds(64 * g + v, 8, stride=8), :] = value

    put(inner, between)
    scaled = [RATE * s for s in between]
    chain = [cut_before(scaled, 1)]
    for v in range(inner):
        chain.append([p * (r + u) for p, r, u in zip(get(forth_ref, v), right[v], chain[-1])])
    after = scaled
    for v in range(inner - 1, -1, -1):
        after = [u + p * x for u, p, x in zip(chain[v + 1], get(forth_ref, v), after)]
        put(v, [x * (1.0 / RATE) for x in after])

    for at, block in turned(lambda s: late_ref[16 * s + 8 : 16 * s + 16, :], index((8, 128), 1)):
        hy_ref[:, at : at + 128] = block
    full = []
    for at, block in turned(lambda s: full_scr[8 * s : 8 * s + 8, :], index((8, 128), 1)):
        e_ref[:, at : at + 128] = block
        full.append(block)
    after = from_after(full, 1, index((ROWS, 128), 1))
    write(hx_ref, [h - RATE * (a - f) for h, a, f in zip(read(half_hx_ref), after, full)])


VMEM = pl.BlockSpec(memory_space=pltpu.VMEM)
SMEM = pl.BlockSpec(memory_space=pltpu.SMEM)
HBM = pl.BlockSpec(memory_space=pltpu.HBM)


def struct(*shape):
    return jax.ShapeDtypeStruct(shape, F32)


def call(kernel, ins, outs, scratch=(), cost=1):
    return pl.pallas_call(
        kernel,
        out_shape=tuple(outs),
        in_specs=list(ins),
        out_specs=(VMEM,) * len(outs),
        scratch_shapes=list(scratch),
        compiler_params=pltpu.CompilerParams(vmem_limit_bytes=32 * 1024 * 1024),
        cost_estimate=pl.CostEstimate(
            flops=cost * 1000000, bytes_accessed=1000, transcendentals=0
        ),
        name=kernel.__name__,
    )


def exchanged(value):
    return lax.all_to_all(value, "xy", split_axis=0, concat_axis=0, tiled=True)


def beside(value):
    count = lax.axis_size("gz")
    sums = []
    for start in (0, 1):
        pairs = []
        for i in range(start, count - 1, 2):
            pairs += [(i, i + 1), (i + 1, i)]
        sums.append(lax.ppermute(value, "gz", pairs))
    return sums


def local(electric, magnetic_first, magnetic_second, region, eps, sig):
    plane = struct(ROWS, LINE)
    packed = struct(PEERS, 8, 128)
    scratch = pltpu.VMEM((ROWS, LINE), F32)
    dma = pltpu.SemaphoreType.DMA
    e = electric.reshape(ROWS, LINE)
    hx = magnetic_first.reshape(ROWS, LINE)
    hy = magnetic_second.reshape(ROWS, LINE)
    region = region.reshape(ROWS, LINE)

    one, two = beside(e)
    e, hx, hy, region = (
        pltpu.with_memory_space_constraint(x, pltpu.HBM) for x in (e, hx, hy, region)
    )
    (below,) = call(
        rows_kernel,
        [HBM] * 2,
        [struct(2, LINE)],
        [pltpu.VMEM((8, LINE), F32), pltpu.VMEM((8, LINE), F32), dma((2,))],
        COSTS["rows"],
    )(e, hx)
    count = lax.axis_size("xy")
    below = lax.ppermute(below, "xy", [(i, (i + 1) % count) for i in range(count)])
    early, dplus, dminus, e, hx = call(
        send_kernel,
        [HBM] * 3 + [SMEM] * 2 + [VMEM],
        [struct(PEERS, 16, 128), plane, plane, plane, plane],
        [pltpu.VMEM((ROWS, LINE), jnp.int32), scratch, dma((3,))],
        COSTS["send"],
    )(region, e, hx, eps, sig, below)
    early = exchanged(early)
    coef, base, hy = call(
        start_kernel,
        [VMEM] * 4 + [HBM, VMEM],
        [struct(2 * LEVELS + 1, ROWS, LINE), plane, plane],
        [dma],
        COSTS["start"],
    )(dplus, dminus, e, hx, hy, below)
    half, half_packed = call(first_kernel, [VMEM] * 4, [plane, packed], (), COSTS["first"])(
        base, one, two, coef
    )
    one, two = beside(half_packed)
    base, full_hy = call(
        between_kernel, [VMEM] * 3, [packed, packed], [scratch] * 2, COSTS["between"]
    )(half, dminus, hy)
    (late,) = call(merge_kernel, [VMEM] * 4, [struct(PEERS, 16, 128)], (), COSTS["merge"])(
        full_hy, base, one, two
    )
    late = exchanged(late)
    rows = 8 * GROUPS
    forth, back, cut, drop, half_hx = call(
        lines_kernel,
        [VMEM],
        [
            struct(SEGMENT - 1, rows, 128),
            struct(SEGMENT - 1, rows, 128),
            struct(2 * CUT_LEVELS + 1, rows, 128),
            struct(SEGMENT, rows, 128),
            plane,
        ],
        (),
        COSTS["lines"],
    )(early.reshape(PEERS * 16, 128))
    out = call(
        second_kernel, [VMEM] * 6, [plane] * 3, [pltpu.VMEM((PEERS * 8, 128), F32)], COSTS["second"]
    )(late.reshape(PEERS * 16, 128), forth, back, cut, drop, half_hx)
    return tuple(o.reshape(1, ROWS, LINE) for o in out)


COSTS = dict(rows=1, send=100000, start=1, first=100000, between=1, merge=1, lines=100000, second=1)


def solution(mesh):
    field = P("gz", "xy", None)
    return jax.shard_map(
        local,
        mesh=mesh,
        in_specs=(field,) * 4 + (P(), P()),
        out_specs=(field,) * 3,
        check_vma=False,
    )
```

profile of v0, /device:TPU:1, one launch (start us, length us, event | category | flops | bytes accessed | tf_op | source)
XLA Modules:
  0.0 70.7 jit_solution(17698559118262335002)
XLA Ops:
  0.6 0.9 %rows_kernel.1 = f32[2,2048]{1,0:T(2,128)S(1)} custom-call(f32[32,2048]{1,0:T(8,128)} %bitcast.13, f32[32,2048]{1,0:T(8,128)} %bitcast.11), custom_call_target="tpu_custom_call" | custom-call | flops 1000000 | bytes 1000 | tf_op jit(solution)/shard_map/rows_kernel/pallas_call | solution.py:475
  1.5 3.1 %collective-permute-start = (f32[2,2048]{1,0:T(2,128)S(1)}, f32[2,2048]{1,0:T(2,128)S(1)}, u32[]{:S(2)}, u32[]{:S(2)}) collective-permute-start(f32[2,2048]{1,0:T(2,128)S(1)} %rows_kernel.1), channel_id=1, source_target_pairs={{0,4},{4,8},{8,12},{12,16},{16,20},{20,24},{24,28},{28,32},{32,36}... | collective-permute-start | bytes 49160 | tf_op jit(solution)/shard_map/ppermute | solution.py:483
  4.6 3.0 %collective-permute-start.1 = (f32[32,2048]{1,0:T(8,128)}, f32[32,2048]{1,0:T(8,128)S(1)}, u32[]{:S(2)}, u32[]{:S(2)}) collective-permute-start(f32[32,2048]{1,0:T(8,128)} %bitcast.14), channel_id=1, source_target_pairs={{0,1},{1,0},{2,3},{3,2},{4,5},{5,4},{6,7},{7,6},{8,9},{9,8},{10,11... | collective-permute-start | bytes 786440 | tf_op jit(solution)/shard_map/ppermute | solution.py:457
  7.6 0.7 collective-permute-start.2
  8.3 0.0 collective-permute-done.below_ref
  8.3 0.0 copy-start
  8.3 0.6 copy-done
  9.0 0.0 copy-start.1
  9.0 0.7 copy-done.1
  9.6 3.9 %send_kernel.1 = (f32[64,16,128]{2,1,0:T(8,128)}, f32[32,2048]{1,0:T(8,128)S(1)}, f32[32,2048]{1,0:T(8,128)S(1)}, f32[32,2048]{1,0:T(8,128)S(1)}, f32[32,2048]{1,0:T(8,128)S(1)}) custom-call(s32[32,2048]{1,0:T(8,128)} %bitcast.18, f32[32,2048]{1,0:T(8,128)} %bitcast.16, f32[32,2048]{1,0:T(8,128)} %bitcast.12, f32[8]{0:T(128)S(1)} %copy-done, ...), custom_call_target="tpu_custom_call" | custom-call | flops 99999997952 | bytes 1000 | tf_op jit(solution)/shard_map/send_kernel/pallas_call | solution.py:484
  13.5 8.0 %all-to-all-start.1 = ((f32[64,16,128]{2,1,0:T(8,128)}), f32[64,16,128]{2,1,0:T(8,128)S(1)}, u32[]{:S(2)}, u32[]{:S(2)}) async-start(f32[64,16,128]{2,1,0:T(8,128)} %get-tuple-element.34), calls=%async_computation.1 | async-start | bytes 1048576 | tf_op jit(solution)/shard_map/all_to_all | solution.py:447
  21.5 2.2 %start_kernel.1 = (f32[23,32,2048]{2,1,0:T(8,128)S(1)}, f32[32,2048]{1,0:T(8,128)S(1)}, f32[32,2048]{1,0:T(8,128)S(1)}) custom-call(f32[32,2048]{1,0:T(8,128)S(1)} %get-tuple-element.23.dplus_ref, f32[32,2048]{1,0:T(8,128)S(1)} %get-tuple-element.24.dminus_ref, f32[32,2048]{1,0:T(8,128)S(1)} %get-tuple-element.25.e_ref, ...), custom_call_target="tpu_custom_call" | custom-call | flops 1000000 | bytes 1000 | tf_op jit(solution)/shard_map/start_kernel/pallas_call | solution.py:492
  23.7 0.0 collective-permute-done.1.up_ref
  23.8 0.0 collective-permute-done.2.down_ref
  23.8 1.9 %first_kernel.1 = (f32[32,2048]{1,0:T(8,128)S(1)}, f32[64,8,128]{2,1,0:T(8,128)S(1)}) custom-call(f32[32,2048]{1,0:T(8,128)S(1)} %get-tuple-element.27.base_ref, f32[32,2048]{1,0:T(8,128)S(1)} %collective-permute-done.1.up_ref, f32[32,2048]{1,0:T(8,128)S(1)} %collective-permute-done.2.down_ref, f32[23,32,2048]{2,1,0:T(8,128)S(1)} %get-tuple-element.28.coef_ref), custom_call_target="tpu_custom_call" | custom-call | flops 99999997952 | bytes 1000 | tf_op jit(solution)/shard_map/first_kernel/pallas_call | solution.py:499
  25.6 6.6 %collective-permute-start.3 = (f32[64,8,128]{2,1,0:T(8,128)S(1)}, f32[64,8,128]{2,1,0:T(8,128)S(1)}, u32[]{:S(2)}, u32[]{:S(2)}) collective-permute-start(f32[64,8,128]{2,1,0:T(8,128)S(1)} %get-tuple-element.33), channel_id=1, source_target_pairs={{0,1},{1,0},{2,3},{3,2},{4,5},{5,4},{6,7},{7,6},{8,9},{9,8},{10,11... | collective-permute-start | bytes 786440 | tf_op jit(solution)/shard_map/ppermute | solution.py:457
  32.2 0.7 collective-permute-start.4
  32.9 2.1 %between_kernel.1 = (f32[64,8,128]{2,1,0:T(8,128)S(1)}, f32[64,8,128]{2,1,0:T(8,128)S(1)}) custom-call(f32[32,2048]{1,0:T(8,128)S(1)} %get-tuple-element.29.half_ref, f32[32,2048]{1,0:T(8,128)S(1)} %get-tuple-element.24.dminus_ref, f32[32,2048]{1,0:T(8,128)S(1)} %get-tuple-element.30.hy_ref), custom_call_target="tpu_custom_call" | custom-call | flops 1000000 | bytes 1000 | tf_op jit(solution)/shard_map/between_kernel/pallas_call | solution.py:503
  35.0 8.8 %collective-permute-done.3.up_ref = f32[64,8,128]{2,1,0:T(8,128)S(1)} collective-permute-done((f32[64,8,128]{2,1,0:T(8,128)S(1)}, f32[64,8,128]{2,1,0:T(8,128)S(1)}, u32[]{:S(2)}, u32[]{:S(2)}) %collective-permute-start.3) | collective-permute-done | bytes 262176 | tf_op jit(solution)/shard_map/ppermute | solution.py:457
  43.8 0.0 collective-permute-done.4.down_ref
  43.8 0.9 %merge_kernel.1 = f32[64,16,128]{2,1,0:T(8,128)} custom-call(f32[64,8,128]{2,1,0:T(8,128)S(1)} %get-tuple-element.31.hy_ref, f32[64,8,128]{2,1,0:T(8,128)S(1)} %get-tuple-element.32.base_ref, f32[64,8,128]{2,1,0:T(8,128)S(1)} %collective-permute-done.3.up_ref, f32[64,8,128]{2,1,0:T(8,128)S(1)} %collective-permute-done.4.down_ref), custom_call_target="tpu_custom_call" | custom-call | flops 1000000 | bytes 1000 | tf_op jit(solution)/shard_map/merge_kernel/pallas_call | solution.py:506
  44.6 0.0 all-to-all-done.1
  44.6 11.1 %all-to-all-start = ((f32[64,16,128]{2,1,0:T(8,128)}), f32[64,16,128]{2,1,0:T(8,128)S(1)}, u32[]{:S(2)}, u32[]{:S(2)}) async-start(f32[64,16,128]{2,1,0:T(8,128)} %merge_kernel.1), calls=%async_computation | async-start | bytes 1048576 | tf_op jit(solution)/shard_map/all_to_all | solution.py:447
  55.8 1.1 %lines_kernel.1 = (f32[7,64,128]{2,1,0:T(8,128)S(1)}, f32[7,64,128]{2,1,0:T(8,128)S(1)}, f32[17,64,128]{2,1,0:T(8,128)S(1)}, f32[8,64,128]{2,1,0:T(8,128)S(1)}, f32[32,2048]{1,0:T(8,128)S(1)}) custom-call(f32[1024,128]{1,0:T(8,128)S(1)} %bitcast.10), custom_call_target="tpu_custom_call" | custom-call | flops 99999997952 | bytes 1000 | tf_op jit(solution)/shard_map/lines_kernel/pallas_call | solution.py:511
  56.9 11.7 %all-to-all-done = f32[64,16,128]{2,1,0:T(8,128)S(1)} async-done(((f32[64,16,128]{2,1,0:T(8,128)}), f32[64,16,128]{2,1,0:T(8,128)S(1)}, u32[]{:S(2)}, u32[]{:S(2)}) %all-to-all-start) | async-done | bytes 524320 | tf_op jit(solution)/shard_map/all_to_all | solution.py:447
  68.6 2.2 %second_kernel.1 = (f32[32,2048]{1,0:T(8,128)}, f32[32,2048]{1,0:T(8,128)}, f32[32,2048]{1,0:T(8,128)}) custom-call(f32[1024,128]{1,0:T(8,128)S(1)} %bitcast.9, f32[7,64,128]{2,1,0:T(8,128)S(1)} %get-tuple-element.35.forth_ref, f32[7,64,128]{2,1,0:T(8,128)S(1)} %get-tuple-element.36.back_ref, f32[17,64,128]{2,1,0:T(8,128)S(1)} %get-tuple-element.37.cut_ref, ...), custom_call_target="tpu_custom_call" | custom-call | flops 1000000 | bytes 1000 | tf_op jit(solution)/shard_map/second_kernel/pallas_call | solution.py:524
Async XLA Ops:
  1.5 6.8 %collective-permute-start = (f32[2,2048]{1,0:T(2,128)S(1)}, f32[2,2048]{1,0:T(2,128)S(1)}, u32[]{:S(2)}, u32[]{:S(2)}) collective-permute-start(f32[2,2048]{1,0:T(2,128)S(1)} %rows_kernel.1), channel_id=1, source_target_pairs={{0,4},{4,8},{8,12},{12,16},{16,20},{20,24},{24,28},{28,32},{32,36}... | collective-permute-start | bytes 49160 | tf_op jit(solution)/shard_map/ppermute | solution.py:483
  4.6 19.1 %collective-permute-start.1 = (f32[32,2048]{1,0:T(8,128)}, f32[32,2048]{1,0:T(8,128)S(1)}, u32[]{:S(2)}, u32[]{:S(2)}) collective-permute-start(f32[32,2048]{1,0:T(8,128)} %bitcast.14), channel_id=1, source_target_pairs={{0,1},{1,0},{2,3},{3,2},{4,5},{5,4},{6,7},{7,6},{8,9},{9,8},{10,11... | collective-permute-start | bytes 786440 | tf_op jit(solution)/shard_map/ppermute | solution.py:457
  7.6 16.1 %collective-permute-start.2 = (f32[32,2048]{1,0:T(8,128)}, f32[32,2048]{1,0:T(8,128)S(1)}, u32[]{:S(2)}, u32[]{:S(2)}) collective-permute-start(f32[32,2048]{1,0:T(8,128)} %bitcast.15), channel_id=1, source_target_pairs={{1,2},{2,1},{5,6},{6,5},{9,10},{10,9},{13,14},{14,13},{17,18},{18,... | collective-permute-start | bytes 786440 | tf_op jit(solution)/shard_map/ppermute | solution.py:457
  8.3 0.7 copy-start
  9.0 0.7 copy-start.1
  13.5 31.1 %all-to-all-start.1 = ((f32[64,16,128]{2,1,0:T(8,128)}), f32[64,16,128]{2,1,0:T(8,128)S(1)}, u32[]{:S(2)}, u32[]{:S(2)}) async-start(f32[64,16,128]{2,1,0:T(8,128)} %get-tuple-element.34), calls=%async_computation.1 | async-start | bytes 1048576 | tf_op jit(solution)/shard_map/all_to_all | solution.py:447
  25.6 18.1 %collective-permute-start.3 = (f32[64,8,128]{2,1,0:T(8,128)S(1)}, f32[64,8,128]{2,1,0:T(8,128)S(1)}, u32[]{:S(2)}, u32[]{:S(2)}) collective-permute-start(f32[64,8,128]{2,1,0:T(8,128)S(1)} %get-tuple-element.33), channel_id=1, source_target_pairs={{0,1},{1,0},{2,3},{3,2},{4,5},{5,4},{6,7},{7,6},{8,9},{9,8},{10,11... | collective-permute-start | bytes 786440 | tf_op jit(solution)/shard_map/ppermute | solution.py:457
  32.2 11.5 %collective-permute-start.4 = (f32[64,8,128]{2,1,0:T(8,128)S(1)}, f32[64,8,128]{2,1,0:T(8,128)S(1)}, u32[]{:S(2)}, u32[]{:S(2)}) collective-permute-start(f32[64,8,128]{2,1,0:T(8,128)S(1)} %get-tuple-element.33), channel_id=1, source_target_pairs={{1,2},{2,1},{5,6},{6,5},{9,10},{10,9},{13,14},{14,13},{17,18},{18,... | collective-permute-start | bytes 786440 | tf_op jit(solution)/shard_map/ppermute | solution.py:457
  44.6 23.9 %all-to-all-start = ((f32[64,16,128]{2,1,0:T(8,128)}), f32[64,16,128]{2,1,0:T(8,128)S(1)}, u32[]{:S(2)}, u32[]{:S(2)}) async-start(f32[64,16,128]{2,1,0:T(8,128)} %merge_kernel.1), calls=%async_computation | async-start | bytes 1048576 | tf_op jit(solution)/shard_map/all_to_all | solution.py:447
where the time goes:
time: 71.1 us; the launch traced here: 70.7 us
  starting transfers between devices  33.1 us (47%)
  waiting for transfers between devices  20.5 us (29%)
  Pallas kernels  15 us (21%)
  local copies, waits for them, and re-layouts  1.31 us (2%)
  between operations  0.75 us (1%)
    all_to_all x2, starting transfers between devices, exchanged(): return lax.all_to_all(value, 'xy', split_axis=0, concat_axis=0, tiled=True)  19.1 us
    all_to_all x2, waiting for transfers between devices, exchanged(): return lax.all_to_all(value, 'xy', split_axis=0, concat_axis=0, tiled=True)  11.7 us
    ppermute x4, starting transfers between devices, beside(): sums.append(lax.ppermute(value, 'gz', pairs))  10.9 us
    ppermute x4, waiting for transfers between devices, beside(): sums.append(lax.ppermute(value, 'gz', pairs))  8.78 us
    pallas_call x1, Pallas kernels, local(): call(send_kernel, [HBM] * 3 + [SMEM] * 2 + [VMEM], [struct(PEERS, 16, 128...  3.86 us
    ppermute x1, starting transfers between devices, local(): lax.ppermute(below, 'xy', [(i, (i + 1) % count) for i in range(count)])  3.1 us
    pallas_call x1, Pallas kernels, local(): call(start_kernel, [VMEM] * 4 + [HBM, VMEM], [struct(2 * LEVELS + 1, ROWS...  2.24 us
    pallas_call x1, Pallas kernels, local(): call(second_kernel, [VMEM] * 6, [plane] * 3, [pltpu.VMEM((PEERS * 8, 128)...  2.16 us
  transfers between devices with their start and end apart: 7, of which 2 were waited for; matrix products, arithmetic and copies ran while one was open for 0% of the time, Pallas kernels for 17%

commit v1 on v0

--- a/solution.py
+++ b/solution.py
@@ -10,6 +10,7 @@
 ROWS = 32
 LINE = 2048
 PEERS = 64
+HALF = ROWS // 2
 TILES = LINE // 128
 F32 = jnp.float32
 LEVELS = 11
@@ -44,6 +45,24 @@
         tiles = [source[8 * u : 8 * u + 8, 128 * q : 128 * q + 128] for u in range(4)]
         for b, tile in enumerate(swap_blocks(tiles, lane)):
             target[4 * q + b, first : first + 8, :] = tile
+
+
+def pack_turned(source, target, first):
+    lane = index((8, 128), 1)
+    for wide in range(4):
+        square = jnp.concatenate(
+            [source[:, 512 * wide + 128 * q : 512 * wide + 128 * q + 128] for q in range(4)], axis=0
+        ).T
+        for b in range(4):
+            tiles = [square[32 * b + 8 * t : 32 * b + 8 * t + 8, :] for t in range(4)]
+            for q, tile in enumerate(swap_blocks(tiles, lane)):
+                target[16 * wide + 4 * q + b, first : first + 8, :] = tile
+
+
+def unpack_turned(tile_of, target, lane):
+    for g in range(TILES):
+        for t, tile in enumerate(swap_blocks([tile_of(4 * g + s) for s in range(4)], lane)):
+            target[8 * t : 8 * t + 8, 128 * g : 128 * g + 128] = tile
 
 
 def turned(tile_of, lane):
@@ -203,32 +222,47 @@
     return [r * w for r, w in zip(right, load(2 * LEVELS))]
 
 
-def rows_kernel(e_ref, hx_ref, below_ref, e_scr, hx_scr, sem):
-    tail = pl.ds(ROWS - 8, 8)
+def rows_kernel(e_hbm, hx_hbm, below_ref, e_ref, hx_ref, sem):
     copies = [
-        pltpu.make_async_copy(hx_ref.at[tail], hx_scr, sem.at[0]),
-        pltpu.make_async_copy(e_ref.at[tail], e_scr, sem.at[1]),
+        pltpu.make_async_copy(e_hbm, e_ref, sem.at[0]),
+        pltpu.make_async_copy(hx_hbm, hx_ref, sem.at[1]),
     ]
     for c in copies:
         c.start()
     for c in copies:
         c.wait()
-    below_ref[0:1, :] = hx_scr[7:8, :]
-    below_ref[1:2, :] = e_scr[7:8, :]
+    below_ref[0:1, :] = hx_ref[ROWS - 1 : ROWS, :]
+    below_ref[1:2, :] = e_ref[ROWS - 1 : ROWS, :]
 
 
 def send_kernel(
-    region_hbm, e_hbm, hx_hbm, eps_ref, sig_ref, below_ref,
-    early_ref, dplus_ref, dminus_ref, e_ref, hx_ref,
-    region_ref, shifted_ref, sem,
+    region_hbm, eps_hbm, sig_hbm, e_ref, hx_ref, below_ref,
+    early_hbm, dplus_ref, dminus_ref,
+    region_ref, eps_ref, sig_ref, shifted_ref, tiles_ref, sem,
 ):
     copies = [
-        pltpu.make_async_copy(region_hbm, region_ref, sem.at[0]),
-        pltpu.make_async_copy(e_hbm, e_ref, sem.at[1]),
-        pltpu.make_async_copy(hx_hbm, hx_ref, sem.at[2]),
+        pltpu.make_async_copy(eps_hbm, eps_ref, sem.at[0]),
+        pltpu.make_async_copy(sig_hbm, sig_ref, sem.at[1]),
+        pltpu.make_async_copy(region_hbm, region_ref, sem.at[2]),
     ]
     for c in copies:
         c.start()
+    row = index((ROWS, 128), 0)
+    inside = lax.axis_index("xy") > 0
+    for k in range(TILES):
+        at = pl.ds(128 * k, 128)
+        e = e_ref[:, at]
+        edge = below_ref[0:1, at] - RATE * (jnp.where(inside, e[0:1], 0.0) - below_ref[1:2, at])
+        half_hx = hx_ref[:, at] - RATE * (pltpu.roll(e, ROWS - 1, 0) - e)
+        shifted_ref[:, at] = jnp.where(row == 0, edge, pltpu.roll(half_hx, 1, 0))
+    pack(shifted_ref, tiles_ref.at[1], 0)
+    sends = [
+        pltpu.make_async_copy(tiles_ref.at[i], early_hbm.at[:, pl.ds(8 * i, 8), :], sem.at[3 + i])
+        for i in range(2)
+    ]
+    sends[1].start()
+    for c in copies:
+        c.wait()
     plus_table = []
     minus_table = []
     for entry in range(8):
@@ -236,10 +270,6 @@
         sig = 0.5 * sig_ref[entry]
         plus_table.append(eps + sig)
         minus_table.append(eps - sig)
-    row = index((ROWS, 128), 0)
-    inside = lax.axis_index("xy") > 0
-    for c in copies:
-        c.wait()
     for k, here in enumerate(read(region_ref)):
         at = pl.ds(128 * k, 128)
         a = jnp.full((ROWS, 128), plus_table[0])
@@ -250,79 +280,115 @@
             b = jnp.where(mask, minus_table[entry], b)
         dplus_ref[:, at] = a
         dminus_ref[:, at] = b
-        e = e_ref[:, at]
-        edge = below_ref[0:1, at] - RATE * (jnp.where(inside, e[0:1], 0.0) - below_ref[1:2, at])
-        half_hx = hx_ref[:, at] - RATE * (pltpu.roll(e, ROWS - 1, 0) - e)
-        shifted_ref[:, at] = jnp.where(row == 0, edge, pltpu.roll(half_hx, 1, 0))
-    pack(dplus_ref, early_ref, 0)
-    pack(shifted_ref, early_ref, 8)
-
-
-def start_kernel(
-    dplus_ref, dminus_ref, e_ref, hx_ref, hy_hbm, below_ref, coef_ref, base_ref, hy_ref, sem
+    pack(dplus_ref, tiles_ref.at[0], 0)
+    sends[0].start()
+    sends[0].wait()
+    sends[1].wait()
+
+
+def base_of(low, lane, dminus_ref, e_ref, hx_ref, hy_ref, below_ref, base_ref):
+    rows = slice(0, HALF) if low else slice(HALF, ROWS)
+    row = index((HALF, 128), 0)
+    inside = lax.axis_index("xy") > 0
+    hy = [hy_ref[rows, 128 * k : 128 * k + 128] for k in range(TILES)]
+    hy_before = from_before(hy, 1, lane)
+    for k in range(TILES):
+        at = slice(128 * k, 128 * k + 128)
+        hx = hx_ref[rows, at]
+        edge = jnp.where(inside, below_ref[0:1, at], 0.0) if low else hx_ref[HALF - 1 : HALF, at]
+        hx_before = jnp.where(row == 0, edge, pltpu.roll(hx, 1, 0))
+        e = e_ref[rows, at]
+        base_ref[:, at] = (
+            dminus_ref[rows, at] * e + (hy[k] - hy_before[k]) - (hx - hx_before) - (2.0 * KAPPA) * e
+        )
+
+
+def diagonal_of(rows, lane, dplus_ref):
+    return [
+        dplus_ref[rows, 128 * k : 128 * k + 128] + (2.0 * RATE if k else jnp.where(lane > 0, 2.0 * RATE, RATE))
+        for k in range(TILES)
+    ]
+
+
+def start_high_kernel(
+    dplus_ref, dminus_ref, e_ref, hx_ref, hy_hbm, coef_ref, base_ref, hy_ref, sem
 ):
     copy = pltpu.make_async_copy(hy_hbm, hy_ref, sem)
     copy.start()
+    lane = index((HALF, 128), 1)
+    factor_lines(diagonal_of(slice(HALF, ROWS), lane, dplus_ref), lane, coef_ref)
+    copy.wait()
+    base_of(False, lane, dminus_ref, e_ref, hx_ref, hy_ref, None, base_ref)
+
+
+def start_low_kernel(
+    dplus_ref, dminus_ref, e_ref, hx_ref, hy_ref, below_ref, done_ref, coef_ref, base_ref
+):
+    lane = index((HALF, 128), 1)
+    factor_lines(diagonal_of(slice(0, HALF), lane, dplus_ref), lane, coef_ref)
+    base_of(True, lane, dminus_ref, e_ref, hx_ref, hy_ref, below_ref, base_ref)
+
+
+def halo(one, two):
+    layer = lax.axis_index("gz")
+    inner = (layer > 0) & (layer < lax.axis_size("gz") - 1)
+    return one + jnp.where(inner, two, 0.0)
+
+
+def half_kernel(low, base_ref, one_ref, two_ref, coef_ref, half_ref):
+    lane = index((HALF, 128), 1)
+    rows = slice(0, HALF) if low else slice(HALF, ROWS)
+    right = []
+    for k in range(TILES):
+        at = slice(128 * k, 128 * k + 128)
+        right.append(base_ref[:, at] + KAPPA * halo(one_ref[rows, at], two_ref[rows, at]))
+    write(half_ref, reduce_lines(right, lane, coef_ref))
+
+
+def high_kernel(*refs):
+    half_kernel(False, *refs)
+
+
+def low_kernel(*refs):
+    half_kernel(True, *refs)
+
+
+def between_kernel(
+    half_low_ref, half_high_ref, dminus_ref, hy_ref, one_ref, two_ref,
+    base_ref, late_hbm, h_scr, tiles_ref, sem,
+):
     lane = index((ROWS, 128), 1)
-    row = index((ROWS, 128), 0)
-    diagonal = [
-        d + (2.0 * RATE if k else jnp.where(lane > 0, 2.0 * RATE, RATE))
-        for k, d in enumerate(read(dplus_ref))
-    ]
-    factor_lines(diagonal, lane, coef_ref)
-    inside = lax.axis_index("xy") > 0
-    copy.wait()
-    hy_before = from_before(read(hy_ref), 1, lane)
-    for k in range(TILES):
-        at = pl.ds(128 * k, 128)
-        hx = hx_ref[:, at]
-        edge = jnp.where(inside, below_ref[0:1, at], 0.0)
-        hx_before = jnp.where(row == 0, edge, pltpu.roll(hx, 1, 0))
-        e = e_ref[:, at]
-        base_ref[:, at] = (
-            dminus_ref[:, at] * e + (hy_ref[:, at] - hy_before[k]) - (hx - hx_before) - (2.0 * KAPPA) * e
-        )
-
-
-def first_kernel(base_ref, up_ref, down_ref, coef_ref, half_ref, packed_ref):
-    lane = index((ROWS, 128), 1)
-    right = [
-        b + KAPPA * (u + d) for b, u, d in zip(read(base_ref), read(up_ref), read(down_ref))
-    ]
-    write(half_ref, reduce_lines(right, lane, coef_ref))
-    pack(half_ref, packed_ref, 0)
-
-
-def between_kernel(half_ref, dminus_ref, hy_ref, base_ref, full_hy_ref, b_scr, h_scr):
-    lane = index((ROWS, 128), 1)
-    half = read(half_ref)
+    half = [jnp.concatenate(pair, axis=0) for pair in zip(read(half_low_ref), read(half_high_ref))]
     change = [RATE * (a - h) for a, h in zip(from_after(half, 1, lane), half)]
     half_hy = [a + b for a, b in zip(read(hy_ref), change)]
     write(h_scr, [a + b for a, b in zip(half_hy, change)])
+    pack_turned(h_scr, tiles_ref, 0)
+    copy = pltpu.make_async_copy(tiles_ref, late_hbm.at[:, pl.ds(8, 8), :], sem)
+    copy.start()
     hy_before = from_before(half_hy, 1, lane)
     for k, (m, h) in enumerate(zip(read(dminus_ref), half)):
-        b_scr[:, 128 * k : 128 * k + 128] = m * h + (half_hy[k] - hy_before[k]) - (2.0 * KAPPA) * h
-    pack(h_scr, full_hy_ref, 0)
-    pack(b_scr, base_ref, 0)
-
-
-def merge_kernel(hy_ref, base_ref, up_ref, down_ref, late_ref):
-    late_ref[:, 0:8, :] = base_ref[...] + KAPPA * (up_ref[...] + down_ref[...])
-    late_ref[:, 8:16, :] = hy_ref[...]
-
-
-def lines_kernel(early_ref, forth_ref, back_ref, cut_ref, drop_ref, hx_ref):
+        at = pl.ds(128 * k, 128)
+        right = m * h + (half_hy[k] - hy_before[k]) - (2.0 * KAPPA) * h
+        base_ref[0:HALF, at] = right[0:HALF]
+        base_ref[HALF:ROWS, at] = right[HALF:ROWS] + KAPPA * halo(one_ref[:, at], two_ref[:, at])
+    copy.wait()
+
+
+def merge_kernel(late_in, base_ref, one_ref, two_ref, late_hbm, r_scr, tiles_ref, sem):
+    r_scr[0:HALF, :] = base_ref[0:HALF, :] + KAPPA * halo(one_ref[...], two_ref[...])
+    r_scr[HALF:ROWS, :] = base_ref[HALF:ROWS, :]
+    pack(r_scr, tiles_ref, 0)
+    copy = pltpu.make_async_copy(tiles_ref, late_hbm.at[:, pl.ds(0, 8), :], sem)
+    copy.start()
+    copy.wait()
+
+
+def lines_kernel(early_ref, forth_ref, back_ref, cut_ref, drop_ref):
     lane = index((8, 128), 1)
     row = index((8, 128), 0)
 
-    def tiles(which):
-        return lambda s: early_ref[16 * s + 8 * which : 16 * s + 8 * which + 8, :]
-
     def cells(which, v):
         return [early_ref[pl.ds(128 * g + 8 * which + v, 8, stride=16), :] for g in range(GROUPS)]
-
-    blocks = [block for _, block in turned(tiles(1), lane)]
-    write(hx_ref, from_after(blocks, 1, index((ROWS, 128), 1), wrap=True))
 
     def put(ref, at, values):
         for g, value in enumerate(values):
@@ -369,8 +435,19 @@
 
 
 def second_kernel(
-    late_ref, forth_ref, back_ref, cut_ref, drop_ref, half_hx_ref, e_ref, hx_ref, hy_ref, full_scr
+    late_ref, forth_ref, back_ref, cut_ref, drop_ref, early_ref, e_hbm, hx_hbm, hy_hbm,
+    full_scr, hx_scr, e_ref, hx_ref, hy_ref, sem,
 ):
+    lane = index((8, 128), 1)
+    unpack_turned(lambda s: late_ref[16 * s + 8 : 16 * s + 16, :], hy_ref, lane)
+    copies = [pltpu.make_async_copy(hy_ref, hy_hbm, sem.at[8])]
+    copies[0].start()
+
+    def after_hx(v):
+        if v == SEGMENT - 1:
+            return cut_after([early_ref[pl.ds(128 * g + 8, 8, stride=16), :] for g in range(GROUPS)], 1, wrap=True)
+        return [early_ref[pl.ds(128 * g + 8 + v + 1, 8, stride=16), :] for g in range(GROUPS)]
+
     def get(ref, at):
         return [ref[at, 8 * g : 8 * g + 8, :] for g in range(GROUPS)]
 
@@ -395,28 +472,35 @@
         )
     between = [r * w for r, w in zip(between, get(cut_ref, 2 * CUT_LEVELS))]
 
-    def put(v, values):
+    def store(ref, v, values):
         for g, value in enumerate(values):
-            full_scr[pl.ds(64 * g + v, 8, stride=8), :] = value
-
-    put(inner, between)
+            ref[pl.ds(64 * g + v, 8, stride=8), :] = value
+
+    store(full_scr, inner, between)
     scaled = [RATE * s for s in between]
     chain = [cut_before(scaled, 1)]
     for v in range(inner):
         chain.append([p * (r + u) for p, r, u in zip(get(forth_ref, v), right[v], chain[-1])])
     after = scaled
     for v in range(inner - 1, -1, -1):
-        after = [u + p * x for u, p, x in zip(chain[v + 1], get(forth_ref, v), after)]
-        put(v, [x * (1.0 / RATE) for x in after])
-
-    for at, block in turned(lambda s: late_ref[16 * s + 8 : 16 * s + 16, :], index((8, 128), 1)):
-        hy_ref[:, at : at + 128] = block
-    full = []
-    for at, block in turned(lambda s: full_scr[8 * s : 8 * s + 8, :], index((8, 128), 1)):
-        e_ref[:, at : at + 128] = block
-        full.append(block)
-    after = from_after(full, 1, index((ROWS, 128), 1))
-    write(hx_ref, [h - RATE * (a - f) for h, a, f in zip(read(half_hx_ref), after, full)])
+        here = [u + p * x for u, p, x in zip(chain[v + 1], get(forth_ref, v), after)]
+        store(full_scr, v, [x * (1.0 / RATE) for x in here])
+        store(hx_scr, v, [h - (a - f) for h, a, f in zip(after_hx(v), after, here)])
+        after = here
+    after = cut_after(after, 1)
+    store(hx_scr, inner, [h - (a - f) for h, a, f in zip(after_hx(inner), after, scaled)])
+
+    for which, (ref, out, source) in enumerate(((e_ref, e_hbm, full_scr), (hx_ref, hx_hbm, hx_scr))):
+        for at, block in turned(lambda s: source[8 * s : 8 * s + 8, :], lane):
+            ref[:, at : at + 128] = block
+            if at % 512 == 384:
+                slab = pl.ds(at - 384, 512)
+                copies.append(
+                    pltpu.make_async_copy(ref.at[:, slab], out.at[:, slab], sem.at[4 * which + at // 512])
+                )
+                copies[-1].start()
+    for copy in copies:
+        copy.wait()
 
 
 VMEM = pl.BlockSpec(memory_space=pltpu.VMEM)
@@ -428,12 +512,13 @@
     return jax.ShapeDtypeStruct(shape, F32)
 
 
-def call(kernel, ins, outs, scratch=(), cost=1):
+def call(kernel, ins, outs, scratch=(), cost=1, places=None, aliases=None):
     return pl.pallas_call(
         kernel,
         out_shape=tuple(outs),
         in_specs=list(ins),
-        out_specs=(VMEM,) * len(outs),
+        out_specs=tuple(places or (VMEM,) * len(outs)),
+        input_output_aliases=aliases or {},
         scratch_shapes=list(scratch),
         compiler_params=pltpu.CompilerParams(vmem_limit_bytes=32 * 1024 * 1024),
         cost_estimate=pl.CostEstimate(
@@ -449,13 +534,10 @@
 
 def beside(value):
     count = lax.axis_size("gz")
-    sums = []
-    for start in (0, 1):
-        pairs = []
-        for i in range(start, count - 1, 2):
-            pairs += [(i, i + 1), (i + 1, i)]
-        sums.append(lax.ppermute(value, "gz", pairs))
-    return sums
+    return [
+        lax.ppermute(value, "gz", [(i, (i + (1 if (i + first) % 2 == 0 else -1)) % count) for i in range(count)])
+        for first in (0, 1)
+    ]
 
 
 def local(electric, magnetic_first, magnetic_second, region, eps, sig):
@@ -468,47 +550,59 @@
     hy = magnetic_second.reshape(ROWS, LINE)
     region = region.reshape(ROWS, LINE)
 
+    e, hx, hy, region, eps, sig = (
+        pltpu.with_memory_space_constraint(x, pltpu.HBM) for x in (e, hx, hy, region, eps, sig)
+    )
+    below, e, hx = call(
+        rows_kernel, [HBM] * 2, [struct(2, LINE), plane, plane], [dma((2,))], COSTS["rows"]
+    )(e, hx)
     one, two = beside(e)
-    e, hx, hy, region = (
-        pltpu.with_memory_space_constraint(x, pltpu.HBM) for x in (e, hx, hy, region)
-    )
-    (below,) = call(
-        rows_kernel,
-        [HBM] * 2,
-        [struct(2, LINE)],
-        [pltpu.VMEM((8, LINE), F32), pltpu.VMEM((8, LINE), F32), dma((2,))],
-        COSTS["rows"],
-    )(e, hx)
     count = lax.axis_size("xy")
     below = lax.ppermute(below, "xy", [(i, (i + 1) % count) for i in range(count)])
-    early, dplus, dminus, e, hx = call(
+    table = pltpu.SMEM((8,), F32)
+    early, dplus, dminus = call(
         send_kernel,
-        [HBM] * 3 + [SMEM] * 2 + [VMEM],
-        [struct(PEERS, 16, 128), plane, plane, plane, plane],
-        [pltpu.VMEM((ROWS, LINE), jnp.int32), scratch, dma((3,))],
+        [HBM] * 3 + [VMEM] * 3,
+        [struct(PEERS, 16, 128), plane, plane],
+        [pltpu.VMEM((ROWS, LINE), jnp.int32), table, table, scratch, pltpu.VMEM((2, PEERS, 8, 128), F32), dma((5,))],
         COSTS["send"],
-    )(region, e, hx, eps, sig, below)
+        [HBM, VMEM, VMEM],
+    )(region, eps, sig, e, hx, below)
     early = exchanged(early)
+    half_plane = struct(HALF, LINE)
+    coefs = struct(2 * LEVELS + 1, HALF, LINE)
     coef, base, hy = call(
-        start_kernel,
-        [VMEM] * 4 + [HBM, VMEM],
-        [struct(2 * LEVELS + 1, ROWS, LINE), plane, plane],
-        [dma],
-        COSTS["start"],
-    )(dplus, dminus, e, hx, hy, below)
-    half, half_packed = call(first_kernel, [VMEM] * 4, [plane, packed], (), COSTS["first"])(
-        base, one, two, coef
+        start_high_kernel, [VMEM] * 4 + [HBM], [coefs, half_plane, plane], [dma], COSTS["start"]
+    )(dplus, dminus, e, hx, hy)
+    (half_high,) = call(high_kernel, [VMEM] * 4, [half_plane], (), COSTS["high"])(base, one, two, coef)
+    high_one, high_two = beside(half_high)
+    coef, base = call(start_low_kernel, [VMEM] * 7, [coefs, half_plane], (), COSTS["startlow"])(
+        dplus, dminus, e, hx, hy, below, half_high
     )
-    one, two = beside(half_packed)
-    base, full_hy = call(
-        between_kernel, [VMEM] * 3, [packed, packed], [scratch] * 2, COSTS["between"]
-    )(half, dminus, hy)
-    (late,) = call(merge_kernel, [VMEM] * 4, [struct(PEERS, 16, 128)], (), COSTS["merge"])(
-        full_hy, base, one, two
-    )
+    (half_low,) = call(low_kernel, [VMEM] * 4, [half_plane], (), COSTS["low"])(base, one, two, coef)
+    low_one, low_two = beside(half_low)
+    tiles = pltpu.VMEM((PEERS, 8, 128), F32)
+    base, late = call(
+        between_kernel,
+        [VMEM] * 6,
+        [plane, struct(PEERS, 16, 128)],
+        [scratch, tiles, dma],
+        COSTS["between"],
+        [VMEM, HBM],
+    )(half_low, half_high, dminus, hy, high_one, high_two)
+    (late,) = call(
+        merge_kernel,
+        [HBM] + [VMEM] * 3,
+        [struct(PEERS, 16, 128)],
+        [scratch, tiles, dma],
+        COSTS["merge"],
+        [HBM],
+        {0: 0},
+    )(late, base, low_one, low_two)
     late = exchanged(late)
     rows = 8 * GROUPS
-    forth, back, cut, drop, half_hx = call(
+    early = early.reshape(PEERS * 16, 128)
+    forth, back, cut, drop = call(
         lines_kernel,
         [VMEM],
         [
@@ -516,18 +610,25 @@
             struct(SEGMENT - 1, rows, 128),
             struct(2 * CUT_LEVELS + 1, rows, 128),
             struct(SEGMENT, rows, 128),
-            plane,
         ],
         (),
         COSTS["lines"],
-    )(early.reshape(PEERS * 16, 128))
+    )(early)
+    tiles = pltpu.VMEM((PEERS * 8, 128), F32)
     out = call(
-        second_kernel, [VMEM] * 6, [plane] * 3, [pltpu.VMEM((PEERS * 8, 128), F32)], COSTS["second"]
-    )(late.reshape(PEERS * 16, 128), forth, back, cut, drop, half_hx)
+        second_kernel,
+        [VMEM] * 6,
+        [plane] * 3,
+        [tiles, tiles, scratch, scratch, scratch, dma((9,))],
+        COSTS["second"],
+        [HBM] * 3,
+    )(
+        late.reshape(PEERS * 16, 128), forth, back, cut, drop, early
+    )
     return tuple(o.reshape(1, ROWS, LINE) for o in out)
 
 
-COSTS = dict(rows=1, send=100000, start=1, first=100000, between=1, merge=1, lines=100000, second=1)
+COSTS = dict(rows=1, send=100000, start=1, startlow=1, high=100000, low=1, between=1, merge=1, lines=100000, second=1)
 
 
 def solution(mesh):

time: 71.1 us -> 67.3 us (0.947)
  Pallas kernels: 15 us -> 12.8 us
  waiting for transfers between devices: 20.5 us -> 18.7 us
  starting transfers between devices: 33.1 us -> 34.8 us
  local copies, waits for them, and re-layouts: 1.31 us -> 0 us
    ppermute x4 -> x6, waiting for transfers between devices: 8.78 us -> 6.43 us  [beside(): lax.ppermute(value, 'gz', [(i, (i + (1 if (i + first) % 2 == 0 else -1))...]
    pallas_call x7 -> x9, Pallas kernels: 14 us -> 12.3 us  [the longest x1 2.41 us: local(): call(second_kernel, [VMEM] * 6, [plane] * 3, [tiles, tiles, scratch, scra...]
    ppermute x4 -> x6, starting transfers between devices: 10.9 us -> 12.4 us  [beside(): lax.ppermute(value, 'gz', [(i, (i + (1 if (i + first) % 2 == 0 else -1))...]
    unnamed x4 -> x0, local copies, waits for them, and re-layouts: 1.31 us -> none
  transfers between devices with their start and end apart: 7 -> 9, of which waited for: 2 -> 4; matrix products, arithmetic and copies ran while one was open for 0% -> 0% of each run, Pallas kernels for 17% -> 14%
where the time goes in v1:
time: 67.3 us; the launch traced here: 67.1 us
  starting transfers between devices  34.8 us (52%)
  waiting for transfers between devices  18.7 us (28%)
  Pallas kernels  12.8 us (19%)
  between operations  0.75 us (1%)
    all_to_all x2, starting transfers between devices, exchanged(): return lax.all_to_all(value, 'xy', split_axis=0, concat_axis=0, tiled=True)  19.3 us
    ppermute x6, starting transfers between devices, beside(): lax.ppermute(value, 'gz', [(i, (i + (1 if (i + first) % 2 == 0 else -1))...  12.4 us
    all_to_all x2, waiting for transfers between devices, exchanged(): return lax.all_to_all(value, 'xy', split_axis=0, concat_axis=0, tiled=True)  12.3 us
    ppermute x6, waiting for transfers between devices, beside(): lax.ppermute(value, 'gz', [(i, (i + (1 if (i + first) % 2 == 0 else -1))...  6.43 us
    ppermute x1, starting transfers between devices, local(): lax.ppermute(below, 'xy', [(i, (i + 1) % count) for i in range(count)])  3.1 us
    pallas_call x1, Pallas kernels, local(): call(second_kernel, [VMEM] * 6, [plane] * 3, [tiles, tiles, scratch, scra...  2.41 us
    pallas_call x1, Pallas kernels, local(): call(send_kernel, [HBM] * 3 + [VMEM] * 3, [struct(PEERS, 16, 128), plane,...  2.17 us
    pallas_call x1, Pallas kernels, local(): call(between_kernel, [VMEM] * 6, [plane, struct(PEERS, 16, 128)], [scratc...  1.65 us
  transfers between devices with their start and end apart: 9, of which 4 were waited for; matrix products, arithmetic and copies ran while one was open for 0% of the time, Pallas kernels for 14%

profile of v1, /device:TPU:1, one launch (start us, length us, event | category | flops | bytes accessed | tf_op | source)
XLA Modules:
  0.0 67.1 jit_solution(10124100287427842668)
XLA Ops:
  0.6 1.1 %rows_kernel.1 = (f32[2,2048]{1,0:T(2,128)S(1)}, f32[32,2048]{1,0:T(8,128)S(1)}, f32[32,2048]{1,0:T(8,128)S(1)}) custom-call(f32[32,2048]{1,0:T(8,128)} %bitcast.13, f32[32,2048]{1,0:T(8,128)} %bitcast.14), custom_call_target="tpu_custom_call" | custom-call | flops 1000000 | bytes 1000 | tf_op jit(solution)/shard_map/rows_kernel/pallas_call | solution.py:556
  1.7 3.1 %collective-permute-start = (f32[2,2048]{1,0:T(2,128)S(1)}, f32[2,2048]{1,0:T(2,128)S(1)}, u32[]{:S(2)}, u32[]{:S(2)}) collective-permute-start(f32[2,2048]{1,0:T(2,128)S(1)} %get-tuple-element.25), channel_id=1, source_target_pairs={{0,4},{4,8},{8,12},{12,16},{16,20},{20,24},{24,28},{28,32},{32,36}... | collective-permute-start | bytes 49160 | tf_op jit(solution)/shard_map/ppermute | solution.py:561
  4.8 3.0 %collective-permute-start.1 = (f32[32,2048]{1,0:T(8,128)S(1)}, f32[32,2048]{1,0:T(8,128)S(1)}, u32[]{:S(2)}, u32[]{:S(2)}) collective-permute-start(f32[32,2048]{1,0:T(8,128)S(1)} %get-tuple-element.23.e_ref), channel_id=1, source_target_pairs={{0,1},{1,0},{2,3},{3,2},{4,5},{5,4},{6,7},{7,6},{8,9},{9,8},{10,11... | collective-permute-start | bytes 786440 | tf_op jit(solution)/shard_map/ppermute | solution.py:538
  7.8 3.3 %collective-permute-start.2 = (f32[32,2048]{1,0:T(8,128)S(1)}, f32[32,2048]{1,0:T(8,128)S(1)}, u32[]{:S(2)}, u32[]{:S(2)}) collective-permute-start(f32[32,2048]{1,0:T(8,128)S(1)} %get-tuple-element.23.e_ref), channel_id=1, source_target_pairs={{0,3},{1,2},{2,1},{3,0},{4,7},{5,6},{6,5},{7,4},{8,11},{9,10},{10,... | collective-permute-start | bytes 786440 | tf_op jit(solution)/shard_map/ppermute | solution.py:538
  11.1 0.0 collective-permute-done.below_ref
  11.1 2.2 %send_kernel.1 = (f32[64,16,128]{2,1,0:T(8,128)}, f32[32,2048]{1,0:T(8,128)S(1)}, f32[32,2048]{1,0:T(8,128)S(1)}) custom-call(s32[32,2048]{1,0:T(8,128)} %bitcast.15, f32[8]{0:T(128)} %eps_hbm.1, f32[8]{0:T(128)} %sig_hbm.1, f32[32,2048]{1,0:T(8,128)S(1)} %get-tuple-element.23.e_ref, f32[32,2048]{1,0:T(8,128)S(1)} %get-tuple-element.24.hx_ref, ...), custom_call_target="tpu_custom_call" | custom-call | flops 99999997952 | bytes 1000 | tf_op jit(solution)/shard_map/send_kernel/pallas_call | solution.py:563
  13.3 8.8 %all-to-all-start.1 = ((f32[64,16,128]{2,1,0:T(8,128)}), f32[64,16,128]{2,1,0:T(8,128)S(1)}, u32[]{:S(2)}, u32[]{:S(2)}) async-start(f32[64,16,128]{2,1,0:T(8,128)} %get-tuple-element.35), calls=%async_computation.1 | async-start | bytes 1048576 | tf_op jit(solution)/shard_map/all_to_all | solution.py:532
  22.1 1.3 %start_high_kernel.1 = (f32[23,16,2048]{2,1,0:T(8,128)S(1)}, f32[16,2048]{1,0:T(8,128)S(1)}, f32[32,2048]{1,0:T(8,128)S(1)}) custom-call(f32[32,2048]{1,0:T(8,128)S(1)} %get-tuple-element.26.dplus_ref, f32[32,2048]{1,0:T(8,128)S(1)} %get-tuple-element.27.dminus_ref, f32[32,2048]{1,0:T(8,128)S(1)} %get-tuple-element.23.e_ref, ...), custom_call_target="tpu_custom_call" | custom-call | flops 1000000 | bytes 1000 | tf_op jit(solution)/shard_map/start_high_kernel/pallas_call | solution.py:574
  23.3 0.0 collective-permute-done.1.refs_1_
  23.3 0.0 collective-permute-done.2.refs_2_
  23.3 0.8 %high_kernel.1.done_ref.half_high_ref = f32[16,2048]{1,0:T(8,128)S(1)} custom-call(f32[16,2048]{1,0:T(8,128)S(1)} %get-tuple-element.29.refs_0_, f32[32,2048]{1,0:T(8,128)S(1)} %collective-permute-done.1.refs_1_, f32[32,2048]{1,0:T(8,128)S(1)} %collective-permute-done.2.refs_2_, f32[23,16,2048]{2,1,0:T(8,128)S(1)} %get-tuple-element.30.refs_3_), custom_call_target="tpu_custom_call" | custom-call | flops 99999997952 | bytes 1000 | tf_op jit(solution)/shard_map/high_kernel/pallas_call | solution.py:577
  24.2 1.3 %collective-permute-start.3 = (f32[16,2048]{1,0:T(8,128)S(1)}, f32[16,2048]{1,0:T(8,128)S(1)}, u32[]{:S(2)}, u32[]{:S(2)}) collective-permute-start(f32[16,2048]{1,0:T(8,128)S(1)} %high_kernel.1.done_ref.half_high_ref), channel_id=1, source_target_pairs={{0,1},{1,0},{2,3},{3,2},{4,5},{5,4},{6,7},{7,6},{8,9},{9,8},{10,11... | collective-permute-start | bytes 393224 | tf_op jit(solution)/shard_map/ppermute | solution.py:538
  25.4 3.5 %collective-permute-start.4 = (f32[16,2048]{1,0:T(8,128)S(1)}, f32[16,2048]{1,0:T(8,128)S(1)}, u32[]{:S(2)}, u32[]{:S(2)}) collective-permute-start(f32[16,2048]{1,0:T(8,128)S(1)} %high_kernel.1.done_ref.half_high_ref), channel_id=1, source_target_pairs={{0,3},{1,2},{2,1},{3,0},{4,7},{5,6},{6,5},{7,4},{8,11},{9,10},{10,... | collective-permute-start | bytes 393224 | tf_op jit(solution)/shard_map/ppermute | solution.py:538
  28.9 1.2 %start_low_kernel.1 = (f32[23,16,2048]{2,1,0:T(8,128)S(1)}, f32[16,2048]{1,0:T(8,128)S(1)}) custom-call(f32[32,2048]{1,0:T(8,128)S(1)} %get-tuple-element.26.dplus_ref, f32[32,2048]{1,0:T(8,128)S(1)} %get-tuple-element.27.dminus_ref, f32[32,2048]{1,0:T(8,128)S(1)} %get-tuple-element.23.e_ref, f32[32,2048]{1,0:T(8,128)S(1)} %get-tuple-element.24.hx_ref, ...), custom_call_target="tpu_custom_call" | custom-call | flops 1000000 | bytes 1000 | tf_op jit(solution)/shard_map/start_low_kernel/pallas_call | solution.py:579
  30.1 0.8 %low_kernel.1.half_low_ref = f32[16,2048]{1,0:T(8,128)S(1)} custom-call(f32[16,2048]{1,0:T(8,128)S(1)} %get-tuple-element.31.refs_0_, f32[32,2048]{1,0:T(8,128)S(1)} %collective-permute-done.1.refs_1_, f32[32,2048]{1,0:T(8,128)S(1)} %collective-permute-done.2.refs_2_, f32[23,16,2048]{2,1,0:T(8,128)S(1)} %get-tuple-element.32.refs_3_), custom_call_target="tpu_custom_call" | custom-call | flops 1000000 | bytes 1000 | tf_op jit(solution)/shard_map/low_kernel/pallas_call | solution.py:582
  30.9 0.2 collective-permute-start.5
  31.1 1.1 %collective-permute-start.6 = (f32[16,2048]{1,0:T(8,128)S(1)}, f32[16,2048]{1,0:T(8,128)S(1)}, u32[]{:S(2)}, u32[]{:S(2)}) collective-permute-start(f32[16,2048]{1,0:T(8,128)S(1)} %low_kernel.1.half_low_ref), channel_id=1, source_target_pairs={{0,3},{1,2},{2,1},{3,0},{4,7},{5,6},{6,5},{7,4},{8,11},{9,10},{10,... | collective-permute-start | bytes 393224 | tf_op jit(solution)/shard_map/ppermute | solution.py:538
  32.3 0.0 collective-permute-done.3.one_ref
  32.3 0.1 collective-permute-done.4.two_ref
  32.4 1.7 %between_kernel.1 = (f32[32,2048]{1,0:T(8,128)S(1)}, f32[64,16,128]{2,1,0:T(8,128)}) custom-call(f32[16,2048]{1,0:T(8,128)S(1)} %low_kernel.1.half_low_ref, f32[16,2048]{1,0:T(8,128)S(1)} %high_kernel.1.done_ref.half_high_ref, f32[32,2048]{1,0:T(8,128)S(1)} %get-tuple-element.27.dminus_ref, f32[32,2048]{1,0:T(8,128)S(1)} %get-tuple-element.28.hy_ref, ...), custom_call_target="tpu_custom_call" | custom-call | flops 1000000 | bytes 1000 | tf_op jit(solution)/shard_map/between_kernel/pallas_call | solution.py:585
  34.1 6.1 %collective-permute-done.5.one_ref = f32[16,2048]{1,0:T(8,128)S(1)} collective-permute-done((f32[16,2048]{1,0:T(8,128)S(1)}, f32[16,2048]{1,0:T(8,128)S(1)}, u32[]{:S(2)}, u32[]{:S(2)}) %collective-permute-start.5) | collective-permute-done | bytes 131104 | tf_op jit(solution)/shard_map/ppermute | solution.py:538
  40.2 0.2 collective-permute-done.6.two_ref
  40.3 1.0 %merge_kernel.1 = f32[64,16,128]{2,1,0:T(8,128)} custom-call(f32[64,16,128]{2,1,0:T(8,128)} %get-tuple-element.33.late_in, f32[32,2048]{1,0:T(8,128)S(1)} %get-tuple-element.34.base_ref, f32[16,2048]{1,0:T(8,128)S(1)} %collective-permute-done.5.one_ref, f32[16,2048]{1,0:T(8,128)S(1)} %collective-permute-done.6.two_ref), custom_call_target="tpu_custom_call", output_to_operand_aliasing={{}: (0, {})} | custom-call | flops 1000000 | bytes 1000 | tf_op jit(solution)/shard_map/merge_kernel/pallas_call | solution.py:593
  41.3 0.0 all-to-all-done.1
  41.4 10.5 %all-to-all-start = ((f32[64,16,128]{2,1,0:T(8,128)}), f32[64,16,128]{2,1,0:T(8,128)S(1)}, u32[]{:S(2)}, u32[]{:S(2)}) async-start(f32[64,16,128]{2,1,0:T(8,128)} %merge_kernel.1), calls=%async_computation | async-start | bytes 1048576 | tf_op jit(solution)/shard_map/all_to_all | solution.py:532
  51.8 0.5 lines_kernel.1
  52.4 12.3 %all-to-all-done = f32[64,16,128]{2,1,0:T(8,128)S(1)} async-done(((f32[64,16,128]{2,1,0:T(8,128)}), f32[64,16,128]{2,1,0:T(8,128)S(1)}, u32[]{:S(2)}, u32[]{:S(2)}) %all-to-all-start) | async-done | bytes 524320 | tf_op jit(solution)/shard_map/all_to_all | solution.py:532
  64.6 2.4 %second_kernel.1 = (f32[32,2048]{1,0:T(8,128)}, f32[32,2048]{1,0:T(8,128)}, f32[32,2048]{1,0:T(8,128)}) custom-call(f32[1024,128]{1,0:T(8,128)S(1)} %bitcast.11, f32[7,64,128]{2,1,0:T(8,128)S(1)} %get-tuple-element.36.forth_ref, f32[7,64,128]{2,1,0:T(8,128)S(1)} %get-tuple-element.37.back_ref, f32[17,64,128]{2,1,0:T(8,128)S(1)} %get-tuple-element.38.cut_ref, ...), custom_call_target="tpu_custom_call" | custom-call | flops 1000000 | bytes 1000 | tf_op jit(solution)/shard_map/second_kernel/pallas_call | solution.py:618
Async XLA Ops:
  1.7 9.4 %collective-permute-start = (f32[2,2048]{1,0:T(2,128)S(1)}, f32[2,2048]{1,0:T(2,128)S(1)}, u32[]{:S(2)}, u32[]{:S(2)}) collective-permute-start(f32[2,2048]{1,0:T(2,128)S(1)} %get-tuple-element.25), channel_id=1, source_target_pairs={{0,4},{4,8},{8,12},{12,16},{16,20},{20,24},{24,28},{28,32},{32,36}... | collective-permute-start | bytes 49160 | tf_op jit(solution)/shard_map/ppermute | solution.py:561
  4.8 18.5 %collective-permute-start.1 = (f32[32,2048]{1,0:T(8,128)S(1)}, f32[32,2048]{1,0:T(8,128)S(1)}, u32[]{:S(2)}, u32[]{:S(2)}) collective-permute-start(f32[32,2048]{1,0:T(8,128)S(1)} %get-tuple-element.23.e_ref), channel_id=1, source_target_pairs={{0,1},{1,0},{2,3},{3,2},{4,5},{5,4},{6,7},{7,6},{8,9},{9,8},{10,11... | collective-permute-start | bytes 786440 | tf_op jit(solution)/shard_map/ppermute | solution.py:538
  7.8 15.6 %collective-permute-start.2 = (f32[32,2048]{1,0:T(8,128)S(1)}, f32[32,2048]{1,0:T(8,128)S(1)}, u32[]{:S(2)}, u32[]{:S(2)}) collective-permute-start(f32[32,2048]{1,0:T(8,128)S(1)} %get-tuple-element.23.e_ref), channel_id=1, source_target_pairs={{0,3},{1,2},{2,1},{3,0},{4,7},{5,6},{6,5},{7,4},{8,11},{9,10},{10,... | collective-permute-start | bytes 786440 | tf_op jit(solution)/shard_map/ppermute | solution.py:538
  13.3 28.1 %all-to-all-start.1 = ((f32[64,16,128]{2,1,0:T(8,128)}), f32[64,16,128]{2,1,0:T(8,128)S(1)}, u32[]{:S(2)}, u32[]{:S(2)}) async-start(f32[64,16,128]{2,1,0:T(8,128)} %get-tuple-element.35), calls=%async_computation.1 | async-start | bytes 1048576 | tf_op jit(solution)/shard_map/all_to_all | solution.py:532
  24.2 8.1 %collective-permute-start.3 = (f32[16,2048]{1,0:T(8,128)S(1)}, f32[16,2048]{1,0:T(8,128)S(1)}, u32[]{:S(2)}, u32[]{:S(2)}) collective-permute-start(f32[16,2048]{1,0:T(8,128)S(1)} %high_kernel.1.done_ref.half_high_ref), channel_id=1, source_target_pairs={{0,1},{1,0},{2,3},{3,2},{4,5},{5,4},{6,7},{7,6},{8,9},{9,8},{10,11... | collective-permute-start | bytes 393224 | tf_op jit(solution)/shard_map/ppermute | solution.py:538
  25.4 7.0 %collective-permute-start.4 = (f32[16,2048]{1,0:T(8,128)S(1)}, f32[16,2048]{1,0:T(8,128)S(1)}, u32[]{:S(2)}, u32[]{:S(2)}) collective-permute-start(f32[16,2048]{1,0:T(8,128)S(1)} %high_kernel.1.done_ref.half_high_ref), channel_id=1, source_target_pairs={{0,3},{1,2},{2,1},{3,0},{4,7},{5,6},{6,5},{7,4},{8,11},{9,10},{10,... | collective-permute-start | bytes 393224 | tf_op jit(solution)/shard_map/ppermute | solution.py:538
  30.9 9.2 %collective-permute-start.5 = (f32[16,2048]{1,0:T(8,128)S(1)}, f32[16,2048]{1,0:T(8,128)S(1)}, u32[]{:S(2)}, u32[]{:S(2)}) collective-permute-start(f32[16,2048]{1,0:T(8,128)S(1)} %low_kernel.1.half_low_ref), channel_id=1, source_target_pairs={{0,1},{1,0},{2,3},{3,2},{4,5},{5,4},{6,7},{7,6},{8,9},{9,8},{10,11... | collective-permute-start | bytes 393224 | tf_op jit(solution)/shard_map/ppermute | solution.py:538
  31.1 9.2 %collective-permute-start.6 = (f32[16,2048]{1,0:T(8,128)S(1)}, f32[16,2048]{1,0:T(8,128)S(1)}, u32[]{:S(2)}, u32[]{:S(2)}) collective-permute-start(f32[16,2048]{1,0:T(8,128)S(1)} %low_kernel.1.half_low_ref), channel_id=1, source_target_pairs={{0,3},{1,2},{2,1},{3,0},{4,7},{5,6},{6,5},{7,4},{8,11},{9,10},{10,... | collective-permute-start | bytes 393224 | tf_op jit(solution)/shard_map/ppermute | solution.py:538
  41.4 23.3 %all-to-all-start = ((f32[64,16,128]{2,1,0:T(8,128)}), f32[64,16,128]{2,1,0:T(8,128)S(1)}, u32[]{:S(2)}, u32[]{:S(2)}) async-start(f32[64,16,128]{2,1,0:T(8,128)} %merge_kernel.1), calls=%async_computation | async-start | bytes 1048576 | tf_op jit(solution)/shard_map/all_to_all | solution.py:532

commit v2 on v1

--- a/solution.py
+++ b/solution.py
@@ -355,32 +355,27 @@
 
 def between_kernel(
     half_low_ref, half_high_ref, dminus_ref, hy_ref, one_ref, two_ref,
-    base_ref, late_hbm, h_scr, tiles_ref, sem,
+    base_ref, full_hy_ref, h_scr,
 ):
     lane = index((ROWS, 128), 1)
     half = [jnp.concatenate(pair, axis=0) for pair in zip(read(half_low_ref), read(half_high_ref))]
     change = [RATE * (a - h) for a, h in zip(from_after(half, 1, lane), half)]
     half_hy = [a + b for a, b in zip(read(hy_ref), change)]
     write(h_scr, [a + b for a, b in zip(half_hy, change)])
-    pack_turned(h_scr, tiles_ref, 0)
-    copy = pltpu.make_async_copy(tiles_ref, late_hbm.at[:, pl.ds(8, 8), :], sem)
-    copy.start()
+    pack_turned(h_scr, full_hy_ref, 0)
     hy_before = from_before(half_hy, 1, lane)
     for k, (m, h) in enumerate(zip(read(dminus_ref), half)):
         at = pl.ds(128 * k, 128)
         right = m * h + (half_hy[k] - hy_before[k]) - (2.0 * KAPPA) * h
         base_ref[0:HALF, at] = right[0:HALF]
         base_ref[HALF:ROWS, at] = right[HALF:ROWS] + KAPPA * halo(one_ref[:, at], two_ref[:, at])
-    copy.wait()
-
-
-def merge_kernel(late_in, base_ref, one_ref, two_ref, late_hbm, r_scr, tiles_ref, sem):
+
+
+def merge_kernel(hy_ref, base_ref, one_ref, two_ref, done_ref, late_ref, r_scr):
+    late_ref[:, 8:16, :] = hy_ref[...]
     r_scr[0:HALF, :] = base_ref[0:HALF, :] + KAPPA * halo(one_ref[...], two_ref[...])
     r_scr[HALF:ROWS, :] = base_ref[HALF:ROWS, :]
-    pack(r_scr, tiles_ref, 0)
-    copy = pltpu.make_async_copy(tiles_ref, late_hbm.at[:, pl.ds(0, 8), :], sem)
-    copy.start()
-    copy.wait()
+    pack(r_scr, late_ref, 0)
 
 
 def lines_kernel(early_ref, forth_ref, back_ref, cut_ref, drop_ref):
@@ -542,7 +537,6 @@
 
 def local(electric, magnetic_first, magnetic_second, region, eps, sig):
     plane = struct(ROWS, LINE)
-    packed = struct(PEERS, 8, 128)
     scratch = pltpu.VMEM((ROWS, LINE), F32)
     dma = pltpu.SemaphoreType.DMA
     e = electric.reshape(ROWS, LINE)
@@ -581,25 +575,9 @@
     )
     (half_low,) = call(low_kernel, [VMEM] * 4, [half_plane], (), COSTS["low"])(base, one, two, coef)
     low_one, low_two = beside(half_low)
-    tiles = pltpu.VMEM((PEERS, 8, 128), F32)
-    base, late = call(
-        between_kernel,
-        [VMEM] * 6,
-        [plane, struct(PEERS, 16, 128)],
-        [scratch, tiles, dma],
-        COSTS["between"],
-        [VMEM, HBM],
+    base, full_hy = call(
+        between_kernel, [VMEM] * 6, [plane, struct(PEERS, 8, 128)], [scratch], COSTS["between"]
     )(half_low, half_high, dminus, hy, high_one, high_two)
-    (late,) = call(
-        merge_kernel,
-        [HBM] + [VMEM] * 3,
-        [struct(PEERS, 16, 128)],
-        [scratch, tiles, dma],
-        COSTS["merge"],
-        [HBM],
-        {0: 0},
-    )(late, base, low_one, low_two)
-    late = exchanged(late)
     rows = 8 * GROUPS
     early = early.reshape(PEERS * 16, 128)
     forth, back, cut, drop = call(
@@ -614,6 +592,10 @@
         (),
         COSTS["lines"],
     )(early)
+    (late,) = call(
+        merge_kernel, [VMEM] * 4 + [HBM], [struct(PEERS, 16, 128)], [scratch], COSTS["merge"]
+    )(full_hy, base, low_one, low_two, drop)
+    late = exchanged(late)
     tiles = pltpu.VMEM((PEERS * 8, 128), F32)
     out = call(
         second_kernel,

time: 67.3 us -> 66.3 us (0.985)
  blocking collectives: 0 us -> 23.1 us
  waiting for transfers between devices: 18.7 us -> 6.61 us
  starting transfers between devices: 34.8 us -> 24.3 us
  Pallas kernels: 12.8 us -> 11.4 us
    all_to_all x0 -> x1, blocking collectives: none -> 23.1 us  [exchanged(): return lax.all_to_all(value, 'xy', split_axis=0, concat_axis=0, tiled=True)]
    all_to_all x2 -> x1, starting transfers between devices: 19.3 us -> 8.77 us  [exchanged(): return lax.all_to_all(value, 'xy', split_axis=0, concat_axis=0, tiled=True)]
    all_to_all x2 -> x1, waiting for transfers between devices: 12.3 us -> 4.68 us  [exchanged(): return lax.all_to_all(value, 'xy', split_axis=0, concat_axis=0, tiled=True)]
    ppermute x6, waiting for transfers between devices: 6.43 us -> 1.92 us  [beside(): lax.ppermute(value, 'gz', [(i, (i + (1 if (i + first) % 2 == 0 else -1))...]
    pallas_call x2, Pallas kernels: 2.64 us -> 1.24 us  [the longest x1 0.97 us: local(): call(between_kernel, [VMEM] * 6, [plane, struct(PEERS, 8, 128)], [scratch...]
  transfers between devices with their start and end apart: 9 -> 8, of which waited for: 4 -> 4; matrix products, arithmetic and copies ran while one was open for 0% -> 0% of each run, Pallas kernels for 14% -> 12%
where the time goes in v2:
time: 66.3 us; the launch traced here: 66.1 us
  starting transfers between devices  24.3 us (37%)
  blocking collectives  23.1 us (35%)
  Pallas kernels  11.4 us (17%)
  waiting for transfers between devices  6.61 us (10%)
  between operations  0.72 us (1%)
    all_to_all x1, blocking collectives, exchanged(): return lax.all_to_all(value, 'xy', split_axis=0, concat_axis=0, tiled=True)  23.1 us
    ppermute x6, starting transfers between devices, beside(): lax.ppermute(value, 'gz', [(i, (i + (1 if (i + first) % 2 == 0 else -1))...  12.4 us
    all_to_all x1, starting transfers between devices, exchanged(): return lax.all_to_all(value, 'xy', split_axis=0, concat_axis=0, tiled=True)  8.77 us
    all_to_all x1, waiting for transfers between devices, exchanged(): return lax.all_to_all(value, 'xy', split_axis=0, concat_axis=0, tiled=True)  4.68 us
    ppermute x1, starting transfers between devices, local(): lax.ppermute(below, 'xy', [(i, (i + 1) % count) for i in range(count)])  3.1 us
    pallas_call x1, Pallas kernels, local(): call(second_kernel, [VMEM] * 6, [plane] * 3, [tiles, tiles, scratch, scra...  2.41 us
    pallas_call x1, Pallas kernels, local(): call(send_kernel, [HBM] * 3 + [VMEM] * 3, [struct(PEERS, 16, 128), plane,...  2.16 us
    ppermute x6, waiting for transfers between devices, beside(): lax.ppermute(value, 'gz', [(i, (i + (1 if (i + first) % 2 == 0 else -1))...  1.92 us
  transfers between devices with their start and end apart: 8, of which 4 were waited for; matrix products, arithmetic and copies ran while one was open for 0% of the time, Pallas kernels for 12%

profile of v2, /device:TPU:1, one launch (start us, length us, event | category | flops | bytes accessed | tf_op | source)
XLA Modules:
  0.0 66.1 jit_solution(3159403110382479388)
XLA Ops:
  0.6 1.1 %rows_kernel.1 = (f32[2,2048]{1,0:T(2,128)S(1)}, f32[32,2048]{1,0:T(8,128)S(1)}, f32[32,2048]{1,0:T(8,128)S(1)}) custom-call(f32[32,2048]{1,0:T(8,128)} %bitcast.13, f32[32,2048]{1,0:T(8,128)} %bitcast.14), custom_call_target="tpu_custom_call" | custom-call | flops 1000000 | bytes 1000 | tf_op jit(solution)/shard_map/rows_kernel/pallas_call | solution.py:550
  1.7 3.1 %collective-permute-start = (f32[2,2048]{1,0:T(2,128)S(1)}, f32[2,2048]{1,0:T(2,128)S(1)}, u32[]{:S(2)}, u32[]{:S(2)}) collective-permute-start(f32[2,2048]{1,0:T(2,128)S(1)} %get-tuple-element.25), channel_id=1, source_target_pairs={{0,4},{4,8},{8,12},{12,16},{16,20},{20,24},{24,28},{28,32},{32,36}... | collective-permute-start | bytes 49160 | tf_op jit(solution)/shard_map/ppermute | solution.py:555
  4.8 3.0 %collective-permute-start.1 = (f32[32,2048]{1,0:T(8,128)S(1)}, f32[32,2048]{1,0:T(8,128)S(1)}, u32[]{:S(2)}, u32[]{:S(2)}) collective-permute-start(f32[32,2048]{1,0:T(8,128)S(1)} %get-tuple-element.23.e_ref), channel_id=1, source_target_pairs={{0,1},{1,0},{2,3},{3,2},{4,5},{5,4},{6,7},{7,6},{8,9},{9,8},{10,11... | collective-permute-start | bytes 786440 | tf_op jit(solution)/shard_map/ppermute | solution.py:533
  7.8 3.3 %collective-permute-start.2 = (f32[32,2048]{1,0:T(8,128)S(1)}, f32[32,2048]{1,0:T(8,128)S(1)}, u32[]{:S(2)}, u32[]{:S(2)}) collective-permute-start(f32[32,2048]{1,0:T(8,128)S(1)} %get-tuple-element.23.e_ref), channel_id=1, source_target_pairs={{0,3},{1,2},{2,1},{3,0},{4,7},{5,6},{6,5},{7,4},{8,11},{9,10},{10,... | collective-permute-start | bytes 786440 | tf_op jit(solution)/shard_map/ppermute | solution.py:533
  11.1 0.0 collective-permute-done.below_ref
  11.1 2.2 %send_kernel.1 = (f32[64,16,128]{2,1,0:T(8,128)}, f32[32,2048]{1,0:T(8,128)S(1)}, f32[32,2048]{1,0:T(8,128)S(1)}) custom-call(s32[32,2048]{1,0:T(8,128)} %bitcast.15, f32[8]{0:T(128)} %eps_hbm.1, f32[8]{0:T(128)} %sig_hbm.1, f32[32,2048]{1,0:T(8,128)S(1)} %get-tuple-element.23.e_ref, f32[32,2048]{1,0:T(8,128)S(1)} %get-tuple-element.24.hx_ref, ...), custom_call_target="tpu_custom_call" | custom-call | flops 99999997952 | bytes 1000 | tf_op jit(solution)/shard_map/send_kernel/pallas_call | solution.py:557
  13.3 8.8 %all-to-all-start = ((f32[64,16,128]{2,1,0:T(8,128)}), f32[64,16,128]{2,1,0:T(8,128)S(1)}, u32[]{:S(2)}, u32[]{:S(2)}) async-start(f32[64,16,128]{2,1,0:T(8,128)} %get-tuple-element.35), calls=%async_computation | async-start | bytes 1048576 | tf_op jit(solution)/shard_map/all_to_all | solution.py:527
  22.0 1.3 %start_high_kernel.1 = (f32[23,16,2048]{2,1,0:T(8,128)S(1)}, f32[16,2048]{1,0:T(8,128)S(1)}, f32[32,2048]{1,0:T(8,128)S(1)}) custom-call(f32[32,2048]{1,0:T(8,128)S(1)} %get-tuple-element.26.dplus_ref, f32[32,2048]{1,0:T(8,128)S(1)} %get-tuple-element.27.dminus_ref, f32[32,2048]{1,0:T(8,128)S(1)} %get-tuple-element.23.e_ref, ...), custom_call_target="tpu_custom_call" | custom-call | flops 1000000 | bytes 1000 | tf_op jit(solution)/shard_map/start_high_kernel/pallas_call | solution.py:568
  23.3 0.0 collective-permute-done.1.refs_1_
  23.3 0.0 collective-permute-done.2.refs_2_
  23.3 0.8 %high_kernel.1.done_ref.half_high_ref = f32[16,2048]{1,0:T(8,128)S(1)} custom-call(f32[16,2048]{1,0:T(8,128)S(1)} %get-tuple-element.29.refs_0_, f32[32,2048]{1,0:T(8,128)S(1)} %collective-permute-done.1.refs_1_, f32[32,2048]{1,0:T(8,128)S(1)} %collective-permute-done.2.refs_2_, f32[23,16,2048]{2,1,0:T(8,128)S(1)} %get-tuple-element.30.refs_3_), custom_call_target="tpu_custom_call" | custom-call | flops 99999997952 | bytes 1000 | tf_op jit(solution)/shard_map/high_kernel/pallas_call | solution.py:571
  24.1 1.3 %collective-permute-start.3 = (f32[16,2048]{1,0:T(8,128)S(1)}, f32[16,2048]{1,0:T(8,128)S(1)}, u32[]{:S(2)}, u32[]{:S(2)}) collective-permute-start(f32[16,2048]{1,0:T(8,128)S(1)} %high_kernel.1.done_ref.half_high_ref), channel_id=1, source_target_pairs={{0,1},{1,0},{2,3},{3,2},{4,5},{5,4},{6,7},{7,6},{8,9},{9,8},{10,11... | collective-permute-start | bytes 393224 | tf_op jit(solution)/shard_map/ppermute | solution.py:533
  25.4 3.5 %collective-permute-start.4 = (f32[16,2048]{1,0:T(8,128)S(1)}, f32[16,2048]{1,0:T(8,128)S(1)}, u32[]{:S(2)}, u32[]{:S(2)}) collective-permute-start(f32[16,2048]{1,0:T(8,128)S(1)} %high_kernel.1.done_ref.half_high_ref), channel_id=1, source_target_pairs={{0,3},{1,2},{2,1},{3,0},{4,7},{5,6},{6,5},{7,4},{8,11},{9,10},{10,... | collective-permute-start | bytes 393224 | tf_op jit(solution)/shard_map/ppermute | solution.py:533
  28.9 1.2 %start_low_kernel.1 = (f32[23,16,2048]{2,1,0:T(8,128)S(1)}, f32[16,2048]{1,0:T(8,128)S(1)}) custom-call(f32[32,2048]{1,0:T(8,128)S(1)} %get-tuple-element.26.dplus_ref, f32[32,2048]{1,0:T(8,128)S(1)} %get-tuple-element.27.dminus_ref, f32[32,2048]{1,0:T(8,128)S(1)} %get-tuple-element.23.e_ref, f32[32,2048]{1,0:T(8,128)S(1)} %get-tuple-element.24.hx_ref, ...), custom_call_target="tpu_custom_call" | custom-call | flops 1000000 | bytes 1000 | tf_op jit(solution)/shard_map/start_low_kernel/pallas_call | solution.py:573
  30.1 0.8 %low_kernel.1.half_low_ref = f32[16,2048]{1,0:T(8,128)S(1)} custom-call(f32[16,2048]{1,0:T(8,128)S(1)} %get-tuple-element.31.refs_0_, f32[32,2048]{1,0:T(8,128)S(1)} %collective-permute-done.1.refs_1_, f32[32,2048]{1,0:T(8,128)S(1)} %collective-permute-done.2.refs_2_, f32[23,16,2048]{2,1,0:T(8,128)S(1)} %get-tuple-element.32.refs_3_), custom_call_target="tpu_custom_call" | custom-call | flops 1000000 | bytes 1000 | tf_op jit(solution)/shard_map/low_kernel/pallas_call | solution.py:576
  30.9 0.2 collective-permute-start.5
  31.1 1.1 %collective-permute-start.6 = (f32[16,2048]{1,0:T(8,128)S(1)}, f32[16,2048]{1,0:T(8,128)S(1)}, u32[]{:S(2)}, u32[]{:S(2)}) collective-permute-start(f32[16,2048]{1,0:T(8,128)S(1)} %low_kernel.1.half_low_ref), channel_id=1, source_target_pairs={{0,3},{1,2},{2,1},{3,0},{4,7},{5,6},{6,5},{7,4},{8,11},{9,10},{10,... | collective-permute-start | bytes 393224 | tf_op jit(solution)/shard_map/ppermute | solution.py:533
  32.3 0.0 collective-permute-done.3.one_ref
  32.3 0.1 collective-permute-done.4.two_ref
  32.4 1.0 %between_kernel.1 = (f32[32,2048]{1,0:T(8,128)S(1)}, f32[64,8,128]{2,1,0:T(8,128)S(1)}) custom-call(f32[16,2048]{1,0:T(8,128)S(1)} %low_kernel.1.half_low_ref, f32[16,2048]{1,0:T(8,128)S(1)} %high_kernel.1.done_ref.half_high_ref, f32[32,2048]{1,0:T(8,128)S(1)} %get-tuple-element.27.dminus_ref, f32[32,2048]{1,0:T(8,128)S(1)} %get-tuple-element.28.hy_ref, ...), custom_call_target="tpu_custom_call" | custom-call | flops 1000000 | bytes 1000 | tf_op jit(solution)/shard_map/between_kernel/pallas_call | solution.py:578
  33.3 4.7 %all-to-all-done = f32[64,16,128]{2,1,0:T(8,128)S(1)} async-done(((f32[64,16,128]{2,1,0:T(8,128)}), f32[64,16,128]{2,1,0:T(8,128)S(1)}, u32[]{:S(2)}, u32[]{:S(2)}) %all-to-all-start) | async-done | bytes 524320 | tf_op jit(solution)/shard_map/all_to_all | solution.py:527
  38.0 0.5 lines_kernel.1
  38.5 1.6 %collective-permute-done.5.one_ref = f32[16,2048]{1,0:T(8,128)S(1)} collective-permute-done((f32[16,2048]{1,0:T(8,128)S(1)}, f32[16,2048]{1,0:T(8,128)S(1)}, u32[]{:S(2)}, u32[]{:S(2)}) %collective-permute-start.5) | collective-permute-done | bytes 131104 | tf_op jit(solution)/shard_map/ppermute | solution.py:533
  40.2 0.2 collective-permute-done.6.two_ref
  40.3 0.3 merge_kernel.1
  40.6 23.1 %all_to_all.10 = f32[64,16,128]{2,1,0:T(8,128)S(1)} all-to-all(f32[64,16,128]{2,1,0:T(8,128)S(1)} %merge_kernel.1), channel_id=1, replica_groups=mesh['xy'=64,'gz'=4] {'xy'}, dimensions={0} | all-to-all | bytes 1048576 | tf_op jit(solution)/shard_map/all_to_all | solution.py:527
  63.7 2.4 %second_kernel.1 = (f32[32,2048]{1,0:T(8,128)}, f32[32,2048]{1,0:T(8,128)}, f32[32,2048]{1,0:T(8,128)}) custom-call(f32[1024,128]{1,0:T(8,128)S(1)} %bitcast.11, f32[7,64,128]{2,1,0:T(8,128)S(1)} %get-tuple-element.37.forth_ref, f32[7,64,128]{2,1,0:T(8,128)S(1)} %get-tuple-element.38.back_ref, f32[17,64,128]{2,1,0:T(8,128)S(1)} %get-tuple-element.39.cut_ref, ...), custom_call_target="tpu_custom_call" | custom-call | flops 1000000 | bytes 1000 | tf_op jit(solution)/shard_map/second_kernel/pallas_call | solution.py:600
Async XLA Ops:
  1.7 9.4 %collective-permute-start = (f32[2,2048]{1,0:T(2,128)S(1)}, f32[2,2048]{1,0:T(2,128)S(1)}, u32[]{:S(2)}, u32[]{:S(2)}) collective-permute-start(f32[2,2048]{1,0:T(2,128)S(1)} %get-tuple-element.25), channel_id=1, source_target_pairs={{0,4},{4,8},{8,12},{12,16},{16,20},{20,24},{24,28},{28,32},{32,36}... | collective-permute-start | bytes 49160 | tf_op jit(solution)/shard_map/ppermute | solution.py:555
  4.8 18.5 %collective-permute-start.1 = (f32[32,2048]{1,0:T(8,128)S(1)}, f32[32,2048]{1,0:T(8,128)S(1)}, u32[]{:S(2)}, u32[]{:S(2)}) collective-permute-start(f32[32,2048]{1,0:T(8,128)S(1)} %get-tuple-element.23.e_ref), channel_id=1, source_target_pairs={{0,1},{1,0},{2,3},{3,2},{4,5},{5,4},{6,7},{7,6},{8,9},{9,8},{10,11... | collective-permute-start | bytes 786440 | tf_op jit(solution)/shard_map/ppermute | solution.py:533
  7.8 15.5 %collective-permute-start.2 = (f32[32,2048]{1,0:T(8,128)S(1)}, f32[32,2048]{1,0:T(8,128)S(1)}, u32[]{:S(2)}, u32[]{:S(2)}) collective-permute-start(f32[32,2048]{1,0:T(8,128)S(1)} %get-tuple-element.23.e_ref), channel_id=1, source_target_pairs={{0,3},{1,2},{2,1},{3,0},{4,7},{5,6},{6,5},{7,4},{8,11},{9,10},{10,... | collective-permute-start | bytes 786440 | tf_op jit(solution)/shard_map/ppermute | solution.py:533
  13.3 24.8 %all-to-all-start = ((f32[64,16,128]{2,1,0:T(8,128)}), f32[64,16,128]{2,1,0:T(8,128)S(1)}, u32[]{:S(2)}, u32[]{:S(2)}) async-start(f32[64,16,128]{2,1,0:T(8,128)} %get-tuple-element.35), calls=%async_computation | async-start | bytes 1048576 | tf_op jit(solution)/shard_map/all_to_all | solution.py:527
  24.1 8.1 %collective-permute-start.3 = (f32[16,2048]{1,0:T(8,128)S(1)}, f32[16,2048]{1,0:T(8,128)S(1)}, u32[]{:S(2)}, u32[]{:S(2)}) collective-permute-start(f32[16,2048]{1,0:T(8,128)S(1)} %high_kernel.1.done_ref.half_high_ref), channel_id=1, source_target_pairs={{0,1},{1,0},{2,3},{3,2},{4,5},{5,4},{6,7},{7,6},{8,9},{9,8},{10,11... | collective-permute-start | bytes 393224 | tf_op jit(solution)/shard_map/ppermute | solution.py:533
  25.4 6.9 %collective-permute-start.4 = (f32[16,2048]{1,0:T(8,128)S(1)}, f32[16,2048]{1,0:T(8,128)S(1)}, u32[]{:S(2)}, u32[]{:S(2)}) collective-permute-start(f32[16,2048]{1,0:T(8,128)S(1)} %high_kernel.1.done_ref.half_high_ref), channel_id=1, source_target_pairs={{0,3},{1,2},{2,1},{3,0},{4,7},{5,6},{6,5},{7,4},{8,11},{9,10},{10,... | collective-permute-start | bytes 393224 | tf_op jit(solution)/shard_map/ppermute | solution.py:533
  30.9 9.2 %collective-permute-start.5 = (f32[16,2048]{1,0:T(8,128)S(1)}, f32[16,2048]{1,0:T(8,128)S(1)}, u32[]{:S(2)}, u32[]{:S(2)}) collective-permute-start(f32[16,2048]{1,0:T(8,128)S(1)} %low_kernel.1.half_low_ref), channel_id=1, source_target_pairs={{0,1},{1,0},{2,3},{3,2},{4,5},{5,4},{6,7},{7,6},{8,9},{9,8},{10,11... | collective-permute-start | bytes 393224 | tf_op jit(solution)/shard_map/ppermute | solution.py:533
  31.1 9.2 %collective-permute-start.6 = (f32[16,2048]{1,0:T(8,128)S(1)}, f32[16,2048]{1,0:T(8,128)S(1)}, u32[]{:S(2)}, u32[]{:S(2)}) collective-permute-start(f32[16,2048]{1,0:T(8,128)S(1)} %low_kernel.1.half_low_ref), channel_id=1, source_target_pairs={{0,3},{1,2},{2,1},{3,0},{4,7},{5,6},{6,5},{7,4},{8,11},{9,10},{10,... | collective-permute-start | bytes 393224 | tf_op jit(solution)/shard_map/ppermute | solution.py:533

commit v3 on v2

--- a/solution.py
+++ b/solution.py
@@ -332,7 +332,7 @@
 def halo(one, two):
     layer = lax.axis_index("gz")
     inner = (layer > 0) & (layer < lax.axis_size("gz") - 1)
-    return one + jnp.where(inner, two, 0.0)
+    return two + jnp.where(inner, one, 0.0)
 
 
 def half_kernel(low, base_ref, one_ref, two_ref, coef_ref, half_ref):
@@ -531,7 +531,7 @@
     count = lax.axis_size("gz")
     return [
         lax.ppermute(value, "gz", [(i, (i + (1 if (i + first) % 2 == 0 else -1)) % count) for i in range(count)])
-        for first in (0, 1)
+        for first in (1, 0)
     ]
 
 

time: 66.3 us -> 65.5 us (0.988)
  blocking collectives: 23.1 us -> 20.5 us
  waiting for transfers between devices: 6.61 us -> 8.44 us
    ppermute x6, waiting for transfers between devices: 1.92 us -> 8.44 us  [beside(): lax.ppermute(value, 'gz', [(i, (i + (1 if (i + first) % 2 == 0 else -1))...]
    all_to_all x1, waiting for transfers between devices: 4.68 us -> 0.01 us  [exchanged(): return lax.all_to_all(value, 'xy', split_axis=0, concat_axis=0, tiled=True)]
    all_to_all x1, blocking collectives: 23.1 us -> 20.5 us  [exchanged(): return lax.all_to_all(value, 'xy', split_axis=0, concat_axis=0, tiled=True)]
where the time goes in v3:
time: 65.5 us; the launch traced here: 65.3 us
  starting transfers between devices  24.3 us (37%)
  blocking collectives  20.5 us (31%)
  Pallas kernels  11.4 us (17%)
  waiting for transfers between devices  8.44 us (13%)
  between operations  0.72 us (1%)
    all_to_all x1, blocking collectives, exchanged(): return lax.all_to_all(value, 'xy', split_axis=0, concat_axis=0, tiled=True)  20.5 us
    ppermute x6, starting transfers between devices, beside(): lax.ppermute(value, 'gz', [(i, (i + (1 if (i + first) % 2 == 0 else -1))...  12.4 us
    all_to_all x1, starting transfers between devices, exchanged(): return lax.all_to_all(value, 'xy', split_axis=0, concat_axis=0, tiled=True)  8.77 us
    ppermute x6, waiting for transfers between devices, beside(): lax.ppermute(value, 'gz', [(i, (i + (1 if (i + first) % 2 == 0 else -1))...  8.44 us
    ppermute x1, starting transfers between devices, local(): lax.ppermute(below, 'xy', [(i, (i + 1) % count) for i in range(count)])  3.1 us
    pallas_call x1, Pallas kernels, local(): call(second_kernel, [VMEM] * 6, [plane] * 3, [tiles, tiles, scratch, scra...  2.41 us
    pallas_call x1, Pallas kernels, local(): call(send_kernel, [HBM] * 3 + [VMEM] * 3, [struct(PEERS, 16, 128), plane,...  2.16 us
  transfers between devices with their start and end apart: 8, of which 4 were waited for; matrix products, arithmetic and copies ran while one was open for 0% of the time, Pallas kernels for 12%

profile of v3, /device:TPU:1, one launch (start us, length us, event | category | flops | bytes accessed | tf_op | source)
XLA Modules:
  0.0 65.3 jit_solution(14476573202359691429)
XLA Ops:
  0.6 1.1 %rows_kernel.1 = (f32[2,2048]{1,0:T(2,128)S(1)}, f32[32,2048]{1,0:T(8,128)S(1)}, f32[32,2048]{1,0:T(8,128)S(1)}) custom-call(f32[32,2048]{1,0:T(8,128)} %bitcast.13, f32[32,2048]{1,0:T(8,128)} %bitcast.14), custom_call_target="tpu_custom_call" | custom-call | flops 1000000 | bytes 1000 | tf_op jit(solution)/shard_map/rows_kernel/pallas_call | solution.py:550
  1.7 3.1 %collective-permute-start = (f32[2,2048]{1,0:T(2,128)S(1)}, f32[2,2048]{1,0:T(2,128)S(1)}, u32[]{:S(2)}, u32[]{:S(2)}) collective-permute-start(f32[2,2048]{1,0:T(2,128)S(1)} %get-tuple-element.25), channel_id=1, source_target_pairs={{0,4},{4,8},{8,12},{12,16},{16,20},{20,24},{24,28},{28,32},{32,36}... | collective-permute-start | bytes 49160 | tf_op jit(solution)/shard_map/ppermute | solution.py:555
  4.8 5.1 %collective-permute-start.1 = (f32[32,2048]{1,0:T(8,128)S(1)}, f32[32,2048]{1,0:T(8,128)S(1)}, u32[]{:S(2)}, u32[]{:S(2)}) collective-permute-start(f32[32,2048]{1,0:T(8,128)S(1)} %get-tuple-element.23.e_ref), channel_id=1, source_target_pairs={{0,3},{1,2},{2,1},{3,0},{4,7},{5,6},{6,5},{7,4},{8,11},{9,10},{10,... | collective-permute-start | bytes 786440 | tf_op jit(solution)/shard_map/ppermute | solution.py:533
  9.9 1.2 %collective-permute-start.2 = (f32[32,2048]{1,0:T(8,128)S(1)}, f32[32,2048]{1,0:T(8,128)S(1)}, u32[]{:S(2)}, u32[]{:S(2)}) collective-permute-start(f32[32,2048]{1,0:T(8,128)S(1)} %get-tuple-element.23.e_ref), channel_id=1, source_target_pairs={{0,1},{1,0},{2,3},{3,2},{4,5},{5,4},{6,7},{7,6},{8,9},{9,8},{10,11... | collective-permute-start | bytes 786440 | tf_op jit(solution)/shard_map/ppermute | solution.py:533
  11.1 0.0 collective-permute-done.below_ref
  11.1 2.2 %send_kernel.1 = (f32[64,16,128]{2,1,0:T(8,128)}, f32[32,2048]{1,0:T(8,128)S(1)}, f32[32,2048]{1,0:T(8,128)S(1)}) custom-call(s32[32,2048]{1,0:T(8,128)} %bitcast.15, f32[8]{0:T(128)} %eps_hbm.1, f32[8]{0:T(128)} %sig_hbm.1, f32[32,2048]{1,0:T(8,128)S(1)} %get-tuple-element.23.e_ref, f32[32,2048]{1,0:T(8,128)S(1)} %get-tuple-element.24.hx_ref, ...), custom_call_target="tpu_custom_call" | custom-call | flops 99999997952 | bytes 1000 | tf_op jit(solution)/shard_map/send_kernel/pallas_call | solution.py:557
  13.3 8.8 %all-to-all-start = ((f32[64,16,128]{2,1,0:T(8,128)}), f32[64,16,128]{2,1,0:T(8,128)S(1)}, u32[]{:S(2)}, u32[]{:S(2)}) async-start(f32[64,16,128]{2,1,0:T(8,128)} %get-tuple-element.35), calls=%async_computation | async-start | bytes 1048576 | tf_op jit(solution)/shard_map/all_to_all | solution.py:527
  22.0 1.3 %start_high_kernel.1 = (f32[23,16,2048]{2,1,0:T(8,128)S(1)}, f32[16,2048]{1,0:T(8,128)S(1)}, f32[32,2048]{1,0:T(8,128)S(1)}) custom-call(f32[32,2048]{1,0:T(8,128)S(1)} %get-tuple-element.26.dplus_ref, f32[32,2048]{1,0:T(8,128)S(1)} %get-tuple-element.27.dminus_ref, f32[32,2048]{1,0:T(8,128)S(1)} %get-tuple-element.23.e_ref, ...), custom_call_target="tpu_custom_call" | custom-call | flops 1000000 | bytes 1000 | tf_op jit(solution)/shard_map/start_high_kernel/pallas_call | solution.py:568
  23.3 0.0 collective-permute-done.1.refs_1_
  23.3 1.3 %collective-permute-done.2.refs_2_ = f32[32,2048]{1,0:T(8,128)S(1)} collective-permute-done((f32[32,2048]{1,0:T(8,128)S(1)}, f32[32,2048]{1,0:T(8,128)S(1)}, u32[]{:S(2)}, u32[]{:S(2)}) %collective-permute-start.2) | collective-permute-done | bytes 262176 | tf_op jit(solution)/shard_map/ppermute | solution.py:533
  24.6 0.8 %high_kernel.1.done_ref.half_high_ref = f32[16,2048]{1,0:T(8,128)S(1)} custom-call(f32[16,2048]{1,0:T(8,128)S(1)} %get-tuple-element.29.refs_0_, f32[32,2048]{1,0:T(8,128)S(1)} %collective-permute-done.1.refs_1_, f32[32,2048]{1,0:T(8,128)S(1)} %collective-permute-done.2.refs_2_, f32[23,16,2048]{2,1,0:T(8,128)S(1)} %get-tuple-element.30.refs_3_), custom_call_target="tpu_custom_call" | custom-call | flops 99999997952 | bytes 1000 | tf_op jit(solution)/shard_map/high_kernel/pallas_call | solution.py:571
  25.4 1.3 %collective-permute-start.3 = (f32[16,2048]{1,0:T(8,128)S(1)}, f32[16,2048]{1,0:T(8,128)S(1)}, u32[]{:S(2)}, u32[]{:S(2)}) collective-permute-start(f32[16,2048]{1,0:T(8,128)S(1)} %high_kernel.1.done_ref.half_high_ref), channel_id=1, source_target_pairs={{0,3},{1,2},{2,1},{3,0},{4,7},{5,6},{6,5},{7,4},{8,11},{9,10},{10,... | collective-permute-start | bytes 393224 | tf_op jit(solution)/shard_map/ppermute | solution.py:533
  26.7 0.0 collective-permute-start.4
  26.7 1.2 %start_low_kernel.1 = (f32[23,16,2048]{2,1,0:T(8,128)S(1)}, f32[16,2048]{1,0:T(8,128)S(1)}) custom-call(f32[32,2048]{1,0:T(8,128)S(1)} %get-tuple-element.26.dplus_ref, f32[32,2048]{1,0:T(8,128)S(1)} %get-tuple-element.27.dminus_ref, f32[32,2048]{1,0:T(8,128)S(1)} %get-tuple-element.23.e_ref, f32[32,2048]{1,0:T(8,128)S(1)} %get-tuple-element.24.hx_ref, ...), custom_call_target="tpu_custom_call" | custom-call | flops 1000000 | bytes 1000 | tf_op jit(solution)/shard_map/start_low_kernel/pallas_call | solution.py:573
  27.9 0.8 %low_kernel.1.half_low_ref = f32[16,2048]{1,0:T(8,128)S(1)} custom-call(f32[16,2048]{1,0:T(8,128)S(1)} %get-tuple-element.31.refs_0_, f32[32,2048]{1,0:T(8,128)S(1)} %collective-permute-done.1.refs_1_, f32[32,2048]{1,0:T(8,128)S(1)} %collective-permute-done.2.refs_2_, f32[23,16,2048]{2,1,0:T(8,128)S(1)} %get-tuple-element.32.refs_3_), custom_call_target="tpu_custom_call" | custom-call | flops 1000000 | bytes 1000 | tf_op jit(solution)/shard_map/low_kernel/pallas_call | solution.py:576
  28.7 3.0 %collective-permute-start.5 = (f32[16,2048]{1,0:T(8,128)S(1)}, f32[16,2048]{1,0:T(8,128)S(1)}, u32[]{:S(2)}, u32[]{:S(2)}) collective-permute-start(f32[16,2048]{1,0:T(8,128)S(1)} %low_kernel.1.half_low_ref), channel_id=1, source_target_pairs={{0,3},{1,2},{2,1},{3,0},{4,7},{5,6},{6,5},{7,4},{8,11},{9,10},{10,... | collective-permute-start | bytes 393224 | tf_op jit(solution)/shard_map/ppermute | solution.py:533
  31.7 1.8 %collective-permute-start.6 = (f32[16,2048]{1,0:T(8,128)S(1)}, f32[16,2048]{1,0:T(8,128)S(1)}, u32[]{:S(2)}, u32[]{:S(2)}) collective-permute-start(f32[16,2048]{1,0:T(8,128)S(1)} %low_kernel.1.half_low_ref), channel_id=1, source_target_pairs={{0,1},{1,0},{2,3},{3,2},{4,5},{5,4},{6,7},{7,6},{8,9},{9,8},{10,11... | collective-permute-start | bytes 393224 | tf_op jit(solution)/shard_map/ppermute | solution.py:533
  33.5 1.4 %collective-permute-done.3.one_ref = f32[16,2048]{1,0:T(8,128)S(1)} collective-permute-done((f32[16,2048]{1,0:T(8,128)S(1)}, f32[16,2048]{1,0:T(8,128)S(1)}, u32[]{:S(2)}, u32[]{:S(2)}) %collective-permute-start.3) | collective-permute-done | bytes 131104 | tf_op jit(solution)/shard_map/ppermute | solution.py:533
  34.9 0.0 collective-permute-done.4.two_ref
  34.9 1.0 %between_kernel.1 = (f32[32,2048]{1,0:T(8,128)S(1)}, f32[64,8,128]{2,1,0:T(8,128)S(1)}) custom-call(f32[16,2048]{1,0:T(8,128)S(1)} %low_kernel.1.half_low_ref, f32[16,2048]{1,0:T(8,128)S(1)} %high_kernel.1.done_ref.half_high_ref, f32[32,2048]{1,0:T(8,128)S(1)} %get-tuple-element.27.dminus_ref, f32[32,2048]{1,0:T(8,128)S(1)} %get-tuple-element.28.hy_ref, ...), custom_call_target="tpu_custom_call" | custom-call | flops 1000000 | bytes 1000 | tf_op jit(solution)/shard_map/between_kernel/pallas_call | solution.py:578
  35.9 0.0 all-to-all-done
  35.9 0.5 lines_kernel.1
  36.4 3.0 %collective-permute-done.5.one_ref = f32[16,2048]{1,0:T(8,128)S(1)} collective-permute-done((f32[16,2048]{1,0:T(8,128)S(1)}, f32[16,2048]{1,0:T(8,128)S(1)}, u32[]{:S(2)}, u32[]{:S(2)}) %collective-permute-start.5) | collective-permute-done | bytes 131104 | tf_op jit(solution)/shard_map/ppermute | solution.py:533
  39.4 2.8 %collective-permute-done.6.two_ref = f32[16,2048]{1,0:T(8,128)S(1)} collective-permute-done((f32[16,2048]{1,0:T(8,128)S(1)}, f32[16,2048]{1,0:T(8,128)S(1)}, u32[]{:S(2)}, u32[]{:S(2)}) %collective-permute-start.6) | collective-permute-done | bytes 131104 | tf_op jit(solution)/shard_map/ppermute | solution.py:533
  42.2 0.3 merge_kernel.1
  42.4 20.5 %all_to_all.10 = f32[64,16,128]{2,1,0:T(8,128)S(1)} all-to-all(f32[64,16,128]{2,1,0:T(8,128)S(1)} %merge_kernel.1), channel_id=1, replica_groups=mesh['xy'=64,'gz'=4] {'xy'}, dimensions={0} | all-to-all | bytes 1048576 | tf_op jit(solution)/shard_map/all_to_all | solution.py:527
  62.9 2.4 %second_kernel.1 = (f32[32,2048]{1,0:T(8,128)}, f32[32,2048]{1,0:T(8,128)}, f32[32,2048]{1,0:T(8,128)}) custom-call(f32[1024,128]{1,0:T(8,128)S(1)} %bitcast.11, f32[7,64,128]{2,1,0:T(8,128)S(1)} %get-tuple-element.37.forth_ref, f32[7,64,128]{2,1,0:T(8,128)S(1)} %get-tuple-element.38.back_ref, f32[17,64,128]{2,1,0:T(8,128)S(1)} %get-tuple-element.39.cut_ref, ...), custom_call_target="tpu_custom_call" | custom-call | flops 1000000 | bytes 1000 | tf_op jit(solution)/shard_map/second_kernel/pallas_call | solution.py:600
Async XLA Ops:
  1.7 9.4 %collective-permute-start = (f32[2,2048]{1,0:T(2,128)S(1)}, f32[2,2048]{1,0:T(2,128)S(1)}, u32[]{:S(2)}, u32[]{:S(2)}) collective-permute-start(f32[2,2048]{1,0:T(2,128)S(1)} %get-tuple-element.25), channel_id=1, source_target_pairs={{0,4},{4,8},{8,12},{12,16},{16,20},{20,24},{24,28},{28,32},{32,36}... | collective-permute-start | bytes 49160 | tf_op jit(solution)/shard_map/ppermute | solution.py:555
  4.8 18.5 %collective-permute-start.1 = (f32[32,2048]{1,0:T(8,128)S(1)}, f32[32,2048]{1,0:T(8,128)S(1)}, u32[]{:S(2)}, u32[]{:S(2)}) collective-permute-start(f32[32,2048]{1,0:T(8,128)S(1)} %get-tuple-element.23.e_ref), channel_id=1, source_target_pairs={{0,3},{1,2},{2,1},{3,0},{4,7},{5,6},{6,5},{7,4},{8,11},{9,10},{10,... | collective-permute-start | bytes 786440 | tf_op jit(solution)/shard_map/ppermute | solution.py:533
  9.9 14.7 %collective-permute-start.2 = (f32[32,2048]{1,0:T(8,128)S(1)}, f32[32,2048]{1,0:T(8,128)S(1)}, u32[]{:S(2)}, u32[]{:S(2)}) collective-permute-start(f32[32,2048]{1,0:T(8,128)S(1)} %get-tuple-element.23.e_ref), channel_id=1, source_target_pairs={{0,1},{1,0},{2,3},{3,2},{4,5},{5,4},{6,7},{7,6},{8,9},{9,8},{10,11... | collective-permute-start | bytes 786440 | tf_op jit(solution)/shard_map/ppermute | solution.py:533
  13.3 22.6 %all-to-all-start = ((f32[64,16,128]{2,1,0:T(8,128)}), f32[64,16,128]{2,1,0:T(8,128)S(1)}, u32[]{:S(2)}, u32[]{:S(2)}) async-start(f32[64,16,128]{2,1,0:T(8,128)} %get-tuple-element.35), calls=%async_computation | async-start | bytes 1048576 | tf_op jit(solution)/shard_map/all_to_all | solution.py:527
  25.4 9.5 %collective-permute-start.3 = (f32[16,2048]{1,0:T(8,128)S(1)}, f32[16,2048]{1,0:T(8,128)S(1)}, u32[]{:S(2)}, u32[]{:S(2)}) collective-permute-start(f32[16,2048]{1,0:T(8,128)S(1)} %high_kernel.1.done_ref.half_high_ref), channel_id=1, source_target_pairs={{0,3},{1,2},{2,1},{3,0},{4,7},{5,6},{6,5},{7,4},{8,11},{9,10},{10,... | collective-permute-start | bytes 393224 | tf_op jit(solution)/shard_map/ppermute | solution.py:533
  26.7 8.2 %collective-permute-start.4 = (f32[16,2048]{1,0:T(8,128)S(1)}, f32[16,2048]{1,0:T(8,128)S(1)}, u32[]{:S(2)}, u32[]{:S(2)}) collective-permute-start(f32[16,2048]{1,0:T(8,128)S(1)} %high_kernel.1.done_ref.half_high_ref), channel_id=1, source_target_pairs={{0,1},{1,0},{2,3},{3,2},{4,5},{5,4},{6,7},{7,6},{8,9},{9,8},{10,11... | collective-permute-start | bytes 393224 | tf_op jit(solution)/shard_map/ppermute | solution.py:533
  28.7 10.6 %collective-permute-start.5 = (f32[16,2048]{1,0:T(8,128)S(1)}, f32[16,2048]{1,0:T(8,128)S(1)}, u32[]{:S(2)}, u32[]{:S(2)}) collective-permute-start(f32[16,2048]{1,0:T(8,128)S(1)} %low_kernel.1.half_low_ref), channel_id=1, source_target_pairs={{0,3},{1,2},{2,1},{3,0},{4,7},{5,6},{6,5},{7,4},{8,11},{9,10},{10,... | collective-permute-start | bytes 393224 | tf_op jit(solution)/shard_map/ppermute | solution.py:533
  31.7 10.5 %collective-permute-start.6 = (f32[16,2048]{1,0:T(8,128)S(1)}, f32[16,2048]{1,0:T(8,128)S(1)}, u32[]{:S(2)}, u32[]{:S(2)}) collective-permute-start(f32[16,2048]{1,0:T(8,128)S(1)} %low_kernel.1.half_low_ref), channel_id=1, source_target_pairs={{0,1},{1,0},{2,3},{3,2},{4,5},{5,4},{6,7},{7,6},{8,9},{9,8},{10,11... | collective-permute-start | bytes 393224 | tf_op jit(solution)/shard_map/ppermute | solution.py:533

commit v4 on v3

--- a/solution.py
+++ b/solution.py
@@ -220,6 +220,27 @@
     for level in range(LEVELS):
         right = reduce_level(right, load(2 * level), load(2 * level + 1), 1 << level, before, after)
     return [r * w for r, w in zip(right, load(2 * LEVELS))]
+
+
+def solve_lines(diagonal, right, lane):
+    def before(values, step):
+        return from_before(values, step, lane)
+
+    def after(values, step):
+        return from_after(values, step, lane)
+
+    square = RATE * RATE
+    weight = [1.0 / d for d in diagonal]
+    share = [RATE * w * r for w, r in zip(weight, right)]
+    low, high = before(weight, 1), after(weight, 1)
+    right = [r + (a + b) for r, a, b in zip(right, before(share, 1), after(share, 1))]
+    diagonal = [d - square * (a + b) for d, a, b in zip(diagonal, low, high)]
+    couple = [square * w for w in low]
+    couple[0] = jnp.where(lane >= 2, couple[0], 0.0)
+    for level in range(1, LEVELS):
+        diagonal, couple, low, high = factor_level(diagonal, couple, 1 << level, before, after)
+        right = reduce_level(right, low, high, 1 << level, before, after)
+    return [r / d for r, d in zip(right, diagonal)]
 
 
 def rows_kernel(e_hbm, hx_hbm, below_ref, e_ref, hx_ref, sem):
@@ -321,36 +342,31 @@
     base_of(False, lane, dminus_ref, e_ref, hx_ref, hy_ref, None, base_ref)
 
 
-def start_low_kernel(
-    dplus_ref, dminus_ref, e_ref, hx_ref, hy_ref, below_ref, done_ref, coef_ref, base_ref
-):
-    lane = index((HALF, 128), 1)
-    factor_lines(diagonal_of(slice(0, HALF), lane, dplus_ref), lane, coef_ref)
-    base_of(True, lane, dminus_ref, e_ref, hx_ref, hy_ref, below_ref, base_ref)
-
-
 def halo(one, two):
     layer = lax.axis_index("gz")
     inner = (layer > 0) & (layer < lax.axis_size("gz") - 1)
     return two + jnp.where(inner, one, 0.0)
 
 
-def half_kernel(low, base_ref, one_ref, two_ref, coef_ref, half_ref):
+def high_kernel(base_ref, one_ref, two_ref, coef_ref, half_ref):
     lane = index((HALF, 128), 1)
-    rows = slice(0, HALF) if low else slice(HALF, ROWS)
     right = []
     for k in range(TILES):
         at = slice(128 * k, 128 * k + 128)
-        right.append(base_ref[:, at] + KAPPA * halo(one_ref[rows, at], two_ref[rows, at]))
+        right.append(base_ref[:, at] + KAPPA * halo(one_ref[HALF:ROWS, at], two_ref[HALF:ROWS, at]))
     write(half_ref, reduce_lines(right, lane, coef_ref))
 
 
-def high_kernel(*refs):
-    half_kernel(False, *refs)
-
-
-def low_kernel(*refs):
-    half_kernel(True, *refs)
+def low_kernel(
+    dplus_ref, dminus_ref, e_ref, hx_ref, hy_ref, below_ref, one_ref, two_ref, done_ref, half_ref, base_ref
+):
+    lane = index((HALF, 128), 1)
+    base_of(True, lane, dminus_ref, e_ref, hx_ref, hy_ref, below_ref, base_ref)
+    right = []
+    for k in range(TILES):
+        at = slice(128 * k, 128 * k + 128)
+        right.append(base_ref[:, at] + KAPPA * halo(one_ref[0:HALF, at], two_ref[0:HALF, at]))
+    write(half_ref, solve_lines(diagonal_of(slice(0, HALF), lane, dplus_ref), right, lane))
 
 
 def between_kernel(
@@ -570,10 +586,9 @@
     )(dplus, dminus, e, hx, hy)
     (half_high,) = call(high_kernel, [VMEM] * 4, [half_plane], (), COSTS["high"])(base, one, two, coef)
     high_one, high_two = beside(half_high)
-    coef, base = call(start_low_kernel, [VMEM] * 7, [coefs, half_plane], (), COSTS["startlow"])(
-        dplus, dminus, e, hx, hy, below, half_high
-    )
-    (half_low,) = call(low_kernel, [VMEM] * 4, [half_plane], (), COSTS["low"])(base, one, two, coef)
+    (half_low,) = call(
+        low_kernel, [VMEM] * 9, [half_plane], [pltpu.VMEM((HALF, LINE), F32)], COSTS["low"]
+    )(dplus, dminus, e, hx, hy, below, one, two, half_high)
     low_one, low_two = beside(half_low)
     base, full_hy = call(
         between_kernel, [VMEM] * 6, [plane, struct(PEERS, 8, 128)], [scratch], COSTS["between"]
@@ -610,7 +625,7 @@
     return tuple(o.reshape(1, ROWS, LINE) for o in out)
 
 
-COSTS = dict(rows=1, send=100000, start=1, startlow=1, high=100000, low=1, between=1, merge=1, lines=100000, second=1)
+COSTS = dict(rows=1, send=100000, start=1, high=100000, low=1, between=1, merge=1, lines=100000, second=1)
 
 
 def solution(mesh):

time: 65.5 us -> 65.6 us (level)
    pallas_call x2 -> x1, Pallas kernels: 1.98 us -> 1.6 us  [local(): call(low_kernel, [VMEM] * 9, [half_plane], [pltpu.VMEM((HALF, LINE), F32)...]
  transfers between devices with their start and end apart: 8 -> 8, of which waited for: 4 -> 4; matrix products, arithmetic and copies ran while one was open for 0% -> 0% of each run, Pallas kernels for 12% -> 11%
where the time goes in v4:
time: 65.6 us; the launch traced here: 65.3 us
  starting transfers between devices  24.3 us (37%)
  blocking collectives  20.9 us (32%)
  Pallas kernels  11 us (17%)
  waiting for transfers between devices  8.42 us (13%)
  between operations  0.72 us (1%)
    all_to_all x1, blocking collectives, exchanged(): return lax.all_to_all(value, 'xy', split_axis=0, concat_axis=0, tiled=True)  20.9 us
    ppermute x6, starting transfers between devices, beside(): lax.ppermute(value, 'gz', [(i, (i + (1 if (i + first) % 2 == 0 else -1))...  12.4 us
    all_to_all x1, starting transfers between devices, exchanged(): return lax.all_to_all(value, 'xy', split_axis=0, concat_axis=0, tiled=True)  8.77 us
    ppermute x6, waiting for transfers between devices, beside(): lax.ppermute(value, 'gz', [(i, (i + (1 if (i + first) % 2 == 0 else -1))...  8.42 us
    ppermute x1, starting transfers between devices, local(): lax.ppermute(below, 'xy', [(i, (i + 1) % count) for i in range(count)])  3.1 us
    pallas_call x1, Pallas kernels, local(): call(second_kernel, [VMEM] * 6, [plane] * 3, [tiles, tiles, scratch, scra...  2.41 us
    pallas_call x1, Pallas kernels, local(): call(send_kernel, [HBM] * 3 + [VMEM] * 3, [struct(PEERS, 16, 128), plane,...  2.16 us
    pallas_call x1, Pallas kernels, local(): call(low_kernel, [VMEM] * 9, [half_plane], [pltpu.VMEM((HALF, LINE), F32)...  1.6 us
  transfers between devices with their start and end apart: 8, of which 4 were waited for; matrix products, arithmetic and copies ran while one was open for 0% of the time, Pallas kernels for 11%

profile of v4, /device:TPU:1, one launch (start us, length us, event | category | flops | bytes accessed | tf_op | source)
XLA Modules:
  0.0 65.3 jit_solution(2302625336779273574)
XLA Ops:
  0.6 1.1 %rows_kernel.1 = (f32[2,2048]{1,0:T(2,128)S(1)}, f32[32,2048]{1,0:T(8,128)S(1)}, f32[32,2048]{1,0:T(8,128)S(1)}) custom-call(f32[32,2048]{1,0:T(8,128)} %bitcast.13, f32[32,2048]{1,0:T(8,128)} %bitcast.14), custom_call_target="tpu_custom_call" | custom-call | flops 1000000 | bytes 1000 | tf_op jit(solution)/shard_map/rows_kernel/pallas_call | solution.py:566
  1.7 3.1 %collective-permute-start = (f32[2,2048]{1,0:T(2,128)S(1)}, f32[2,2048]{1,0:T(2,128)S(1)}, u32[]{:S(2)}, u32[]{:S(2)}) collective-permute-start(f32[2,2048]{1,0:T(2,128)S(1)} %get-tuple-element.23), channel_id=1, source_target_pairs={{0,4},{4,8},{8,12},{12,16},{16,20},{20,24},{24,28},{28,32},{32,36}... | collective-permute-start | bytes 49160 | tf_op jit(solution)/shard_map/ppermute | solution.py:571
  4.8 5.1 %collective-permute-start.1 = (f32[32,2048]{1,0:T(8,128)S(1)}, f32[32,2048]{1,0:T(8,128)S(1)}, u32[]{:S(2)}, u32[]{:S(2)}) collective-permute-start(f32[32,2048]{1,0:T(8,128)S(1)} %get-tuple-element.21.e_ref), channel_id=1, source_target_pairs={{0,3},{1,2},{2,1},{3,0},{4,7},{5,6},{6,5},{7,4},{8,11},{9,10},{10,... | collective-permute-start | bytes 786440 | tf_op jit(solution)/shard_map/ppermute | solution.py:549
  9.9 1.2 %collective-permute-start.2 = (f32[32,2048]{1,0:T(8,128)S(1)}, f32[32,2048]{1,0:T(8,128)S(1)}, u32[]{:S(2)}, u32[]{:S(2)}) collective-permute-start(f32[32,2048]{1,0:T(8,128)S(1)} %get-tuple-element.21.e_ref), channel_id=1, source_target_pairs={{0,1},{1,0},{2,3},{3,2},{4,5},{5,4},{6,7},{7,6},{8,9},{9,8},{10,11... | collective-permute-start | bytes 786440 | tf_op jit(solution)/shard_map/ppermute | solution.py:549
  11.1 0.0 collective-permute-done.below_ref
  11.1 2.2 %send_kernel.1 = (f32[64,16,128]{2,1,0:T(8,128)}, f32[32,2048]{1,0:T(8,128)S(1)}, f32[32,2048]{1,0:T(8,128)S(1)}) custom-call(s32[32,2048]{1,0:T(8,128)} %bitcast.15, f32[8]{0:T(128)} %eps_hbm.1, f32[8]{0:T(128)} %sig_hbm.1, f32[32,2048]{1,0:T(8,128)S(1)} %get-tuple-element.21.e_ref, f32[32,2048]{1,0:T(8,128)S(1)} %get-tuple-element.22.hx_ref, ...), custom_call_target="tpu_custom_call" | custom-call | flops 99999997952 | bytes 1000 | tf_op jit(solution)/shard_map/send_kernel/pallas_call | solution.py:573
  13.3 8.8 %all-to-all-start = ((f32[64,16,128]{2,1,0:T(8,128)}), f32[64,16,128]{2,1,0:T(8,128)S(1)}, u32[]{:S(2)}, u32[]{:S(2)}) async-start(f32[64,16,128]{2,1,0:T(8,128)} %get-tuple-element.31), calls=%async_computation | async-start | bytes 1048576 | tf_op jit(solution)/shard_map/all_to_all | solution.py:543
  22.0 1.3 %start_high_kernel.1 = (f32[23,16,2048]{2,1,0:T(8,128)S(1)}, f32[16,2048]{1,0:T(8,128)S(1)}, f32[32,2048]{1,0:T(8,128)S(1)}) custom-call(f32[32,2048]{1,0:T(8,128)S(1)} %get-tuple-element.24.dplus_ref, f32[32,2048]{1,0:T(8,128)S(1)} %get-tuple-element.25.dminus_ref, f32[32,2048]{1,0:T(8,128)S(1)} %get-tuple-element.21.e_ref, ...), custom_call_target="tpu_custom_call" | custom-call | flops 1000000 | bytes 1000 | tf_op jit(solution)/shard_map/start_high_kernel/pallas_call | solution.py:584
  23.3 0.0 collective-permute-done.1.one_ref
  23.3 1.3 %collective-permute-done.2.two_ref = f32[32,2048]{1,0:T(8,128)S(1)} collective-permute-done((f32[32,2048]{1,0:T(8,128)S(1)}, f32[32,2048]{1,0:T(8,128)S(1)}, u32[]{:S(2)}, u32[]{:S(2)}) %collective-permute-start.2) | collective-permute-done | bytes 262176 | tf_op jit(solution)/shard_map/ppermute | solution.py:549
  24.6 0.8 %high_kernel.1.done_ref.half_high_ref = f32[16,2048]{1,0:T(8,128)S(1)} custom-call(f32[16,2048]{1,0:T(8,128)S(1)} %get-tuple-element.27.base_ref, f32[32,2048]{1,0:T(8,128)S(1)} %collective-permute-done.1.one_ref, f32[32,2048]{1,0:T(8,128)S(1)} %collective-permute-done.2.two_ref, f32[23,16,2048]{2,1,0:T(8,128)S(1)} %get-tuple-element.28.coef_ref), custom_call_target="tpu_custom_call" | custom-call | flops 99999997952 | bytes 1000 | tf_op jit(solution)/shard_map/high_kernel/pallas_call | solution.py:587
  25.4 1.3 %collective-permute-start.3 = (f32[16,2048]{1,0:T(8,128)S(1)}, f32[16,2048]{1,0:T(8,128)S(1)}, u32[]{:S(2)}, u32[]{:S(2)}) collective-permute-start(f32[16,2048]{1,0:T(8,128)S(1)} %high_kernel.1.done_ref.half_high_ref), channel_id=1, source_target_pairs={{0,3},{1,2},{2,1},{3,0},{4,7},{5,6},{6,5},{7,4},{8,11},{9,10},{10,... | collective-permute-start | bytes 393224 | tf_op jit(solution)/shard_map/ppermute | solution.py:549
  26.7 0.0 collective-permute-start.4
  26.7 1.6 %low_kernel.1.half_low_ref = f32[16,2048]{1,0:T(8,128)S(1)} custom-call(f32[32,2048]{1,0:T(8,128)S(1)} %get-tuple-element.24.dplus_ref, f32[32,2048]{1,0:T(8,128)S(1)} %get-tuple-element.25.dminus_ref, f32[32,2048]{1,0:T(8,128)S(1)} %get-tuple-element.21.e_ref, f32[32,2048]{1,0:T(8,128)S(1)} %get-tuple-element.22.hx_ref, ...), custom_call_target="tpu_custom_call" | custom-call | flops 1000000 | bytes 1000 | tf_op jit(solution)/shard_map/low_kernel/pallas_call | solution.py:589
  28.3 3.0 %collective-permute-start.5 = (f32[16,2048]{1,0:T(8,128)S(1)}, f32[16,2048]{1,0:T(8,128)S(1)}, u32[]{:S(2)}, u32[]{:S(2)}) collective-permute-start(f32[16,2048]{1,0:T(8,128)S(1)} %low_kernel.1.half_low_ref), channel_id=1, source_target_pairs={{0,3},{1,2},{2,1},{3,0},{4,7},{5,6},{6,5},{7,4},{8,11},{9,10},{10,... | collective-permute-start | bytes 393224 | tf_op jit(solution)/shard_map/ppermute | solution.py:549
  31.3 1.8 %collective-permute-start.6 = (f32[16,2048]{1,0:T(8,128)S(1)}, f32[16,2048]{1,0:T(8,128)S(1)}, u32[]{:S(2)}, u32[]{:S(2)}) collective-permute-start(f32[16,2048]{1,0:T(8,128)S(1)} %low_kernel.1.half_low_ref), channel_id=1, source_target_pairs={{0,1},{1,0},{2,3},{3,2},{4,5},{5,4},{6,7},{7,6},{8,9},{9,8},{10,11... | collective-permute-start | bytes 393224 | tf_op jit(solution)/shard_map/ppermute | solution.py:549
  33.1 1.8 %collective-permute-done.3.one_ref = f32[16,2048]{1,0:T(8,128)S(1)} collective-permute-done((f32[16,2048]{1,0:T(8,128)S(1)}, f32[16,2048]{1,0:T(8,128)S(1)}, u32[]{:S(2)}, u32[]{:S(2)}) %collective-permute-start.3) | collective-permute-done | bytes 131104 | tf_op jit(solution)/shard_map/ppermute | solution.py:549
  34.9 0.0 collective-permute-done.4.two_ref
  34.9 1.0 %between_kernel.1 = (f32[32,2048]{1,0:T(8,128)S(1)}, f32[64,8,128]{2,1,0:T(8,128)S(1)}) custom-call(f32[16,2048]{1,0:T(8,128)S(1)} %low_kernel.1.half_low_ref, f32[16,2048]{1,0:T(8,128)S(1)} %high_kernel.1.done_ref.half_high_ref, f32[32,2048]{1,0:T(8,128)S(1)} %get-tuple-element.25.dminus_ref, f32[32,2048]{1,0:T(8,128)S(1)} %get-tuple-element.26.hy_ref, ...), custom_call_target="tpu_custom_call" | custom-call | flops 1000000 | bytes 1000 | tf_op jit(solution)/shard_map/between_kernel/pallas_call | solution.py:593
  35.9 0.0 all-to-all-done
  35.9 0.5 lines_kernel.1
  36.4 2.7 %collective-permute-done.5.one_ref = f32[16,2048]{1,0:T(8,128)S(1)} collective-permute-done((f32[16,2048]{1,0:T(8,128)S(1)}, f32[16,2048]{1,0:T(8,128)S(1)}, u32[]{:S(2)}, u32[]{:S(2)}) %collective-permute-start.5) | collective-permute-done | bytes 131104 | tf_op jit(solution)/shard_map/ppermute | solution.py:549
  39.1 2.6 %collective-permute-done.6.two_ref = f32[16,2048]{1,0:T(8,128)S(1)} collective-permute-done((f32[16,2048]{1,0:T(8,128)S(1)}, f32[16,2048]{1,0:T(8,128)S(1)}, u32[]{:S(2)}, u32[]{:S(2)}) %collective-permute-start.6) | collective-permute-done | bytes 131104 | tf_op jit(solution)/shard_map/ppermute | solution.py:549
  41.8 0.3 merge_kernel.1
  42.0 20.9 %all_to_all.10 = f32[64,16,128]{2,1,0:T(8,128)S(1)} all-to-all(f32[64,16,128]{2,1,0:T(8,128)S(1)} %merge_kernel.1), channel_id=1, replica_groups=mesh['xy'=64,'gz'=4] {'xy'}, dimensions={0} | all-to-all | bytes 1048576 | tf_op jit(solution)/shard_map/all_to_all | solution.py:543
  62.9 2.4 %second_kernel.1 = (f32[32,2048]{1,0:T(8,128)}, f32[32,2048]{1,0:T(8,128)}, f32[32,2048]{1,0:T(8,128)}) custom-call(f32[1024,128]{1,0:T(8,128)S(1)} %bitcast.11, f32[7,64,128]{2,1,0:T(8,128)S(1)} %get-tuple-element.33.forth_ref, f32[7,64,128]{2,1,0:T(8,128)S(1)} %get-tuple-element.34.back_ref, f32[17,64,128]{2,1,0:T(8,128)S(1)} %get-tuple-element.35.cut_ref, ...), custom_call_target="tpu_custom_call" | custom-call | flops 1000000 | bytes 1000 | tf_op jit(solution)/shard_map/second_kernel/pallas_call | solution.py:615
Async XLA Ops:
  1.7 9.4 %collective-permute-start = (f32[2,2048]{1,0:T(2,128)S(1)}, f32[2,2048]{1,0:T(2,128)S(1)}, u32[]{:S(2)}, u32[]{:S(2)}) collective-permute-start(f32[2,2048]{1,0:T(2,128)S(1)} %get-tuple-element.23), channel_id=1, source_target_pairs={{0,4},{4,8},{8,12},{12,16},{16,20},{20,24},{24,28},{28,32},{32,36}... | collective-permute-start | bytes 49160 | tf_op jit(solution)/shard_map/ppermute | solution.py:571
  4.8 18.5 %collective-permute-start.1 = (f32[32,2048]{1,0:T(8,128)S(1)}, f32[32,2048]{1,0:T(8,128)S(1)}, u32[]{:S(2)}, u32[]{:S(2)}) collective-permute-start(f32[32,2048]{1,0:T(8,128)S(1)} %get-tuple-element.21.e_ref), channel_id=1, source_target_pairs={{0,3},{1,2},{2,1},{3,0},{4,7},{5,6},{6,5},{7,4},{8,11},{9,10},{10,... | collective-permute-start | bytes 786440 | tf_op jit(solution)/shard_map/ppermute | solution.py:549
  9.9 14.7 %collective-permute-start.2 = (f32[32,2048]{1,0:T(8,128)S(1)}, f32[32,2048]{1,0:T(8,128)S(1)}, u32[]{:S(2)}, u32[]{:S(2)}) collective-permute-start(f32[32,2048]{1,0:T(8,128)S(1)} %get-tuple-element.21.e_ref), channel_id=1, source_target_pairs={{0,1},{1,0},{2,3},{3,2},{4,5},{5,4},{6,7},{7,6},{8,9},{9,8},{10,11... | collective-permute-start | bytes 786440 | tf_op jit(solution)/shard_map/ppermute | solution.py:549
  13.3 22.6 %all-to-all-start = ((f32[64,16,128]{2,1,0:T(8,128)}), f32[64,16,128]{2,1,0:T(8,128)S(1)}, u32[]{:S(2)}, u32[]{:S(2)}) async-start(f32[64,16,128]{2,1,0:T(8,128)} %get-tuple-element.31), calls=%async_computation | async-start | bytes 1048576 | tf_op jit(solution)/shard_map/all_to_all | solution.py:543
  25.4 9.5 %collective-permute-start.3 = (f32[16,2048]{1,0:T(8,128)S(1)}, f32[16,2048]{1,0:T(8,128)S(1)}, u32[]{:S(2)}, u32[]{:S(2)}) collective-permute-start(f32[16,2048]{1,0:T(8,128)S(1)} %high_kernel.1.done_ref.half_high_ref), channel_id=1, source_target_pairs={{0,3},{1,2},{2,1},{3,0},{4,7},{5,6},{6,5},{7,4},{8,11},{9,10},{10,... | collective-permute-start | bytes 393224 | tf_op jit(solution)/shard_map/ppermute | solution.py:549
  26.7 8.2 %collective-permute-start.4 = (f32[16,2048]{1,0:T(8,128)S(1)}, f32[16,2048]{1,0:T(8,128)S(1)}, u32[]{:S(2)}, u32[]{:S(2)}) collective-permute-start(f32[16,2048]{1,0:T(8,128)S(1)} %high_kernel.1.done_ref.half_high_ref), channel_id=1, source_target_pairs={{0,1},{1,0},{2,3},{3,2},{4,5},{5,4},{6,7},{7,6},{8,9},{9,8},{10,11... | collective-permute-start | bytes 393224 | tf_op jit(solution)/shard_map/ppermute | solution.py:549
  28.3 10.8 %collective-permute-start.5 = (f32[16,2048]{1,0:T(8,128)S(1)}, f32[16,2048]{1,0:T(8,128)S(1)}, u32[]{:S(2)}, u32[]{:S(2)}) collective-permute-start(f32[16,2048]{1,0:T(8,128)S(1)} %low_kernel.1.half_low_ref), channel_id=1, source_target_pairs={{0,3},{1,2},{2,1},{3,0},{4,7},{5,6},{6,5},{7,4},{8,11},{9,10},{10,... | collective-permute-start | bytes 393224 | tf_op jit(solution)/shard_map/ppermute | solution.py:549
  31.3 10.4 %collective-permute-start.6 = (f32[16,2048]{1,0:T(8,128)S(1)}, f32[16,2048]{1,0:T(8,128)S(1)}, u32[]{:S(2)}, u32[]{:S(2)}) collective-permute-start(f32[16,2048]{1,0:T(8,128)S(1)} %low_kernel.1.half_low_ref), channel_id=1, source_target_pairs={{0,1},{1,0},{2,3},{3,2},{4,5},{5,4},{6,7},{7,6},{8,9},{9,8},{10,11... | collective-permute-start | bytes 393224 | tf_op jit(solution)/shard_map/ppermute | solution.py:549

commit v5 on v4

--- a/solution.py
+++ b/solution.py
@@ -39,11 +39,11 @@
     return out
 
 
-def pack(source, target, first):
+def pack(source, target, first, tiles=range(TILES)):
     lane = index((8, 128), 1)
-    for q in range(TILES):
-        tiles = [source[8 * u : 8 * u + 8, 128 * q : 128 * q + 128] for u in range(4)]
-        for b, tile in enumerate(swap_blocks(tiles, lane)):
+    for q in tiles:
+        blocks = [source[8 * u : 8 * u + 8, 128 * q : 128 * q + 128] for u in range(4)]
+        for b, tile in enumerate(swap_blocks(blocks, lane)):
             target[4 * q + b, first : first + 8, :] = tile
 
 
@@ -277,11 +277,8 @@
         half_hx = hx_ref[:, at] - RATE * (pltpu.roll(e, ROWS - 1, 0) - e)
         shifted_ref[:, at] = jnp.where(row == 0, edge, pltpu.roll(half_hx, 1, 0))
     pack(shifted_ref, tiles_ref.at[1], 0)
-    sends = [
-        pltpu.make_async_copy(tiles_ref.at[i], early_hbm.at[:, pl.ds(8 * i, 8), :], sem.at[3 + i])
-        for i in range(2)
-    ]
-    sends[1].start()
+    sends = [pltpu.make_async_copy(tiles_ref.at[1], early_hbm.at[:, pl.ds(8, 8), :], sem.at[3])]
+    sends[0].start()
     for c in copies:
         c.wait()
     plus_table = []
@@ -291,20 +288,26 @@
         sig = 0.5 * sig_ref[entry]
         plus_table.append(eps + sig)
         minus_table.append(eps - sig)
-    for k, here in enumerate(read(region_ref)):
-        at = pl.ds(128 * k, 128)
-        a = jnp.full((ROWS, 128), plus_table[0])
-        b = jnp.full((ROWS, 128), minus_table[0])
-        for entry in range(1, 8):
-            mask = here == entry
-            a = jnp.where(mask, plus_table[entry], a)
-            b = jnp.where(mask, minus_table[entry], b)
-        dplus_ref[:, at] = a
-        dminus_ref[:, at] = b
-    pack(dplus_ref, tiles_ref.at[0], 0)
-    sends[0].start()
-    sends[0].wait()
-    sends[1].wait()
+    for part in range(2):
+        for k in range(8 * part, 8 * part + 8):
+            at = pl.ds(128 * k, 128)
+            here = region_ref[:, at]
+            a = jnp.full((ROWS, 128), plus_table[0])
+            b = jnp.full((ROWS, 128), minus_table[0])
+            for entry in range(1, 8):
+                mask = here == entry
+                a = jnp.where(mask, plus_table[entry], a)
+                b = jnp.where(mask, minus_table[entry], b)
+            dplus_ref[:, at] = a
+            dminus_ref[:, at] = b
+        pack(dplus_ref, tiles_ref.at[0], 0, range(8 * part, 8 * part + 8))
+        where = pl.ds(PEERS // 2 * part, PEERS // 2)
+        sends.append(
+            pltpu.make_async_copy(tiles_ref.at[0, where], early_hbm.at[where, pl.ds(0, 8), :], sem.at[4 + part])
+        )
+        sends[-1].start()
+    for c in sends:
+        c.wait()
 
 
 def base_of(low, lane, dminus_ref, e_ref, hx_ref, hy_ref, below_ref, base_ref):
@@ -574,7 +577,7 @@
         send_kernel,
         [HBM] * 3 + [VMEM] * 3,
         [struct(PEERS, 16, 128), plane, plane],
-        [pltpu.VMEM((ROWS, LINE), jnp.int32), table, table, scratch, pltpu.VMEM((2, PEERS, 8, 128), F32), dma((5,))],
+        [pltpu.VMEM((ROWS, LINE), jnp.int32), table, table, scratch, pltpu.VMEM((2, PEERS, 8, 128), F32), dma((6,))],
         COSTS["send"],
         [HBM, VMEM, VMEM],
     )(region, eps, sig, e, hx, below)

time: 65.6 us -> 65.5 us (level)
  no operation moved by 1% of the time
where the time goes in v5:
time: 65.5 us; the launch traced here: 65.3 us
  starting transfers between devices  24.3 us (37%)
  blocking collectives  20.8 us (32%)
  Pallas kernels  11 us (17%)
  waiting for transfers between devices  8.44 us (13%)
  between operations  0.72 us (1%)
    all_to_all x1, blocking collectives, exchanged(): return lax.all_to_all(value, 'xy', split_axis=0, concat_axis=0, tiled=True)  20.8 us
    ppermute x6, starting transfers between devices, beside(): lax.ppermute(value, 'gz', [(i, (i + (1 if (i + first) % 2 == 0 else -1))...  12.4 us
    all_to_all x1, starting transfers between devices, exchanged(): return lax.all_to_all(value, 'xy', split_axis=0, concat_axis=0, tiled=True)  8.77 us
    ppermute x6, waiting for transfers between devices, beside(): lax.ppermute(value, 'gz', [(i, (i + (1 if (i + first) % 2 == 0 else -1))...  8.43 us
    ppermute x1, starting transfers between devices, local(): lax.ppermute(below, 'xy', [(i, (i + 1) % count) for i in range(count)])  3.1 us
    pallas_call x1, Pallas kernels, local(): call(second_kernel, [VMEM] * 6, [plane] * 3, [tiles, tiles, scratch, scra...  2.41 us
    pallas_call x1, Pallas kernels, local(): call(send_kernel, [HBM] * 3 + [VMEM] * 3, [struct(PEERS, 16, 128), plane,...  2.13 us
    pallas_call x1, Pallas kernels, local(): call(low_kernel, [VMEM] * 9, [half_plane], [pltpu.VMEM((HALF, LINE), F32)...  1.6 us
  transfers between devices with their start and end apart: 8, of which 4 were waited for; matrix products, arithmetic and copies ran while one was open for 0% of the time, Pallas kernels for 11%

profile of v5, /device:TPU:1, one launch (start us, length us, event | category | flops | bytes accessed | tf_op | source)
XLA Modules:
  0.0 65.3 jit_solution(11478248619949858355)
XLA Ops:
  0.6 1.1 %rows_kernel.1 = (f32[2,2048]{1,0:T(2,128)S(1)}, f32[32,2048]{1,0:T(8,128)S(1)}, f32[32,2048]{1,0:T(8,128)S(1)}) custom-call(f32[32,2048]{1,0:T(8,128)} %bitcast.13, f32[32,2048]{1,0:T(8,128)} %bitcast.14), custom_call_target="tpu_custom_call" | custom-call | flops 1000000 | bytes 1000 | tf_op jit(solution)/shard_map/rows_kernel/pallas_call | solution.py:569
  1.7 3.1 %collective-permute-start = (f32[2,2048]{1,0:T(2,128)S(1)}, f32[2,2048]{1,0:T(2,128)S(1)}, u32[]{:S(2)}, u32[]{:S(2)}) collective-permute-start(f32[2,2048]{1,0:T(2,128)S(1)} %get-tuple-element.23), channel_id=1, source_target_pairs={{0,4},{4,8},{8,12},{12,16},{16,20},{20,24},{24,28},{28,32},{32,36}... | collective-permute-start | bytes 49160 | tf_op jit(solution)/shard_map/ppermute | solution.py:574
  4.8 5.1 %collective-permute-start.1 = (f32[32,2048]{1,0:T(8,128)S(1)}, f32[32,2048]{1,0:T(8,128)S(1)}, u32[]{:S(2)}, u32[]{:S(2)}) collective-permute-start(f32[32,2048]{1,0:T(8,128)S(1)} %get-tuple-element.21.e_ref), channel_id=1, source_target_pairs={{0,3},{1,2},{2,1},{3,0},{4,7},{5,6},{6,5},{7,4},{8,11},{9,10},{10,... | collective-permute-start | bytes 786440 | tf_op jit(solution)/shard_map/ppermute | solution.py:552
  9.9 1.2 %collective-permute-start.2 = (f32[32,2048]{1,0:T(8,128)S(1)}, f32[32,2048]{1,0:T(8,128)S(1)}, u32[]{:S(2)}, u32[]{:S(2)}) collective-permute-start(f32[32,2048]{1,0:T(8,128)S(1)} %get-tuple-element.21.e_ref), channel_id=1, source_target_pairs={{0,1},{1,0},{2,3},{3,2},{4,5},{5,4},{6,7},{7,6},{8,9},{9,8},{10,11... | collective-permute-start | bytes 786440 | tf_op jit(solution)/shard_map/ppermute | solution.py:552
  11.1 0.0 collective-permute-done.below_ref
  11.1 2.1 %send_kernel.1 = (f32[64,16,128]{2,1,0:T(8,128)}, f32[32,2048]{1,0:T(8,128)S(1)}, f32[32,2048]{1,0:T(8,128)S(1)}) custom-call(s32[32,2048]{1,0:T(8,128)} %bitcast.15, f32[8]{0:T(128)} %eps_hbm.1, f32[8]{0:T(128)} %sig_hbm.1, f32[32,2048]{1,0:T(8,128)S(1)} %get-tuple-element.21.e_ref, f32[32,2048]{1,0:T(8,128)S(1)} %get-tuple-element.22.hx_ref, ...), custom_call_target="tpu_custom_call" | custom-call | flops 99999997952 | bytes 1000 | tf_op jit(solution)/shard_map/send_kernel/pallas_call | solution.py:576
  13.2 8.8 %all-to-all-start = ((f32[64,16,128]{2,1,0:T(8,128)}), f32[64,16,128]{2,1,0:T(8,128)S(1)}, u32[]{:S(2)}, u32[]{:S(2)}) async-start(f32[64,16,128]{2,1,0:T(8,128)} %get-tuple-element.31), calls=%async_computation | async-start | bytes 1048576 | tf_op jit(solution)/shard_map/all_to_all | solution.py:546
  22.0 1.3 %start_high_kernel.1 = (f32[23,16,2048]{2,1,0:T(8,128)S(1)}, f32[16,2048]{1,0:T(8,128)S(1)}, f32[32,2048]{1,0:T(8,128)S(1)}) custom-call(f32[32,2048]{1,0:T(8,128)S(1)} %get-tuple-element.24.dplus_ref, f32[32,2048]{1,0:T(8,128)S(1)} %get-tuple-element.25.dminus_ref, f32[32,2048]{1,0:T(8,128)S(1)} %get-tuple-element.21.e_ref, ...), custom_call_target="tpu_custom_call" | custom-call | flops 1000000 | bytes 1000 | tf_op jit(solution)/shard_map/start_high_kernel/pallas_call | solution.py:587
  23.3 0.0 collective-permute-done.1.one_ref
  23.3 1.3 %collective-permute-done.2.two_ref = f32[32,2048]{1,0:T(8,128)S(1)} collective-permute-done((f32[32,2048]{1,0:T(8,128)S(1)}, f32[32,2048]{1,0:T(8,128)S(1)}, u32[]{:S(2)}, u32[]{:S(2)}) %collective-permute-start.2) | collective-permute-done | bytes 262176 | tf_op jit(solution)/shard_map/ppermute | solution.py:552
  24.6 0.8 %high_kernel.1.done_ref.half_high_ref = f32[16,2048]{1,0:T(8,128)S(1)} custom-call(f32[16,2048]{1,0:T(8,128)S(1)} %get-tuple-element.27.base_ref, f32[32,2048]{1,0:T(8,128)S(1)} %collective-permute-done.1.one_ref, f32[32,2048]{1,0:T(8,128)S(1)} %collective-permute-done.2.two_ref, f32[23,16,2048]{2,1,0:T(8,128)S(1)} %get-tuple-element.28.coef_ref), custom_call_target="tpu_custom_call" | custom-call | flops 99999997952 | bytes 1000 | tf_op jit(solution)/shard_map/high_kernel/pallas_call | solution.py:590
  25.4 1.3 %collective-permute-start.3 = (f32[16,2048]{1,0:T(8,128)S(1)}, f32[16,2048]{1,0:T(8,128)S(1)}, u32[]{:S(2)}, u32[]{:S(2)}) collective-permute-start(f32[16,2048]{1,0:T(8,128)S(1)} %high_kernel.1.done_ref.half_high_ref), channel_id=1, source_target_pairs={{0,3},{1,2},{2,1},{3,0},{4,7},{5,6},{6,5},{7,4},{8,11},{9,10},{10,... | collective-permute-start | bytes 393224 | tf_op jit(solution)/shard_map/ppermute | solution.py:552
  26.7 0.0 collective-permute-start.4
  26.7 1.6 %low_kernel.1.half_low_ref = f32[16,2048]{1,0:T(8,128)S(1)} custom-call(f32[32,2048]{1,0:T(8,128)S(1)} %get-tuple-element.24.dplus_ref, f32[32,2048]{1,0:T(8,128)S(1)} %get-tuple-element.25.dminus_ref, f32[32,2048]{1,0:T(8,128)S(1)} %get-tuple-element.21.e_ref, f32[32,2048]{1,0:T(8,128)S(1)} %get-tuple-element.22.hx_ref, ...), custom_call_target="tpu_custom_call" | custom-call | flops 1000000 | bytes 1000 | tf_op jit(solution)/shard_map/low_kernel/pallas_call | solution.py:592
  28.3 3.0 %collective-permute-start.5 = (f32[16,2048]{1,0:T(8,128)S(1)}, f32[16,2048]{1,0:T(8,128)S(1)}, u32[]{:S(2)}, u32[]{:S(2)}) collective-permute-start(f32[16,2048]{1,0:T(8,128)S(1)} %low_kernel.1.half_low_ref), channel_id=1, source_target_pairs={{0,3},{1,2},{2,1},{3,0},{4,7},{5,6},{6,5},{7,4},{8,11},{9,10},{10,... | collective-permute-start | bytes 393224 | tf_op jit(solution)/shard_map/ppermute | solution.py:552
  31.3 1.8 %collective-permute-start.6 = (f32[16,2048]{1,0:T(8,128)S(1)}, f32[16,2048]{1,0:T(8,128)S(1)}, u32[]{:S(2)}, u32[]{:S(2)}) collective-permute-start(f32[16,2048]{1,0:T(8,128)S(1)} %low_kernel.1.half_low_ref), channel_id=1, source_target_pairs={{0,1},{1,0},{2,3},{3,2},{4,5},{5,4},{6,7},{7,6},{8,9},{9,8},{10,11... | collective-permute-start | bytes 393224 | tf_op jit(solution)/shard_map/ppermute | solution.py:552
  33.1 1.8 %collective-permute-done.3.one_ref = f32[16,2048]{1,0:T(8,128)S(1)} collective-permute-done((f32[16,2048]{1,0:T(8,128)S(1)}, f32[16,2048]{1,0:T(8,128)S(1)}, u32[]{:S(2)}, u32[]{:S(2)}) %collective-permute-start.3) | collective-permute-done | bytes 131104 | tf_op jit(solution)/shard_map/ppermute | solution.py:552
  34.9 0.0 collective-permute-done.4.two_ref
  34.9 1.0 %between_kernel.1 = (f32[32,2048]{1,0:T(8,128)S(1)}, f32[64,8,128]{2,1,0:T(8,128)S(1)}) custom-call(f32[16,2048]{1,0:T(8,128)S(1)} %low_kernel.1.half_low_ref, f32[16,2048]{1,0:T(8,128)S(1)} %high_kernel.1.done_ref.half_high_ref, f32[32,2048]{1,0:T(8,128)S(1)} %get-tuple-element.25.dminus_ref, f32[32,2048]{1,0:T(8,128)S(1)} %get-tuple-element.26.hy_ref, ...), custom_call_target="tpu_custom_call" | custom-call | flops 1000000 | bytes 1000 | tf_op jit(solution)/shard_map/between_kernel/pallas_call | solution.py:596
  35.9 0.0 all-to-all-done
  35.9 0.5 lines_kernel.1
  36.4 2.7 %collective-permute-done.5.one_ref = f32[16,2048]{1,0:T(8,128)S(1)} collective-permute-done((f32[16,2048]{1,0:T(8,128)S(1)}, f32[16,2048]{1,0:T(8,128)S(1)}, u32[]{:S(2)}, u32[]{:S(2)}) %collective-permute-start.5) | collective-permute-done | bytes 131104 | tf_op jit(solution)/shard_map/ppermute | solution.py:552
  39.1 2.7 %collective-permute-done.6.two_ref = f32[16,2048]{1,0:T(8,128)S(1)} collective-permute-done((f32[16,2048]{1,0:T(8,128)S(1)}, f32[16,2048]{1,0:T(8,128)S(1)}, u32[]{:S(2)}, u32[]{:S(2)}) %collective-permute-start.6) | collective-permute-done | bytes 131104 | tf_op jit(solution)/shard_map/ppermute | solution.py:552
  41.8 0.3 merge_kernel.1
  42.0 20.8 %all_to_all.10 = f32[64,16,128]{2,1,0:T(8,128)S(1)} all-to-all(f32[64,16,128]{2,1,0:T(8,128)S(1)} %merge_kernel.1), channel_id=1, replica_groups=mesh['xy'=64,'gz'=4] {'xy'}, dimensions={0} | all-to-all | bytes 1048576 | tf_op jit(solution)/shard_map/all_to_all | solution.py:546
  62.9 2.4 %second_kernel.1 = (f32[32,2048]{1,0:T(8,128)}, f32[32,2048]{1,0:T(8,128)}, f32[32,2048]{1,0:T(8,128)}) custom-call(f32[1024,128]{1,0:T(8,128)S(1)} %bitcast.11, f32[7,64,128]{2,1,0:T(8,128)S(1)} %get-tuple-element.33.forth_ref, f32[7,64,128]{2,1,0:T(8,128)S(1)} %get-tuple-element.34.back_ref, f32[17,64,128]{2,1,0:T(8,128)S(1)} %get-tuple-element.35.cut_ref, ...), custom_call_target="tpu_custom_call" | custom-call | flops 1000000 | bytes 1000 | tf_op jit(solution)/shard_map/second_kernel/pallas_call | solution.py:618
Async XLA Ops:
  1.7 9.4 %collective-permute-start = (f32[2,2048]{1,0:T(2,128)S(1)}, f32[2,2048]{1,0:T(2,128)S(1)}, u32[]{:S(2)}, u32[]{:S(2)}) collective-permute-start(f32[2,2048]{1,0:T(2,128)S(1)} %get-tuple-element.23), channel_id=1, source_target_pairs={{0,4},{4,8},{8,12},{12,16},{16,20},{20,24},{24,28},{28,32},{32,36}... | collective-permute-start | bytes 49160 | tf_op jit(solution)/shard_map/ppermute | solution.py:574
  4.8 18.5 %collective-permute-start.1 = (f32[32,2048]{1,0:T(8,128)S(1)}, f32[32,2048]{1,0:T(8,128)S(1)}, u32[]{:S(2)}, u32[]{:S(2)}) collective-permute-start(f32[32,2048]{1,0:T(8,128)S(1)} %get-tuple-element.21.e_ref), channel_id=1, source_target_pairs={{0,3},{1,2},{2,1},{3,0},{4,7},{5,6},{6,5},{7,4},{8,11},{9,10},{10,... | collective-permute-start | bytes 786440 | tf_op jit(solution)/shard_map/ppermute | solution.py:552
  9.9 14.7 %collective-permute-start.2 = (f32[32,2048]{1,0:T(8,128)S(1)}, f32[32,2048]{1,0:T(8,128)S(1)}, u32[]{:S(2)}, u32[]{:S(2)}) collective-permute-start(f32[32,2048]{1,0:T(8,128)S(1)} %get-tuple-element.21.e_ref), channel_id=1, source_target_pairs={{0,1},{1,0},{2,3},{3,2},{4,5},{5,4},{6,7},{7,6},{8,9},{9,8},{10,11... | collective-permute-start | bytes 786440 | tf_op jit(solution)/shard_map/ppermute | solution.py:552
  13.2 22.6 %all-to-all-start = ((f32[64,16,128]{2,1,0:T(8,128)}), f32[64,16,128]{2,1,0:T(8,128)S(1)}, u32[]{:S(2)}, u32[]{:S(2)}) async-start(f32[64,16,128]{2,1,0:T(8,128)} %get-tuple-element.31), calls=%async_computation | async-start | bytes 1048576 | tf_op jit(solution)/shard_map/all_to_all | solution.py:546
  25.4 9.5 %collective-permute-start.3 = (f32[16,2048]{1,0:T(8,128)S(1)}, f32[16,2048]{1,0:T(8,128)S(1)}, u32[]{:S(2)}, u32[]{:S(2)}) collective-permute-start(f32[16,2048]{1,0:T(8,128)S(1)} %high_kernel.1.done_ref.half_high_ref), channel_id=1, source_target_pairs={{0,3},{1,2},{2,1},{3,0},{4,7},{5,6},{6,5},{7,4},{8,11},{9,10},{10,... | collective-permute-start | bytes 393224 | tf_op jit(solution)/shard_map/ppermute | solution.py:552
  26.7 8.2 %collective-permute-start.4 = (f32[16,2048]{1,0:T(8,128)S(1)}, f32[16,2048]{1,0:T(8,128)S(1)}, u32[]{:S(2)}, u32[]{:S(2)}) collective-permute-start(f32[16,2048]{1,0:T(8,128)S(1)} %high_kernel.1.done_ref.half_high_ref), channel_id=1, source_target_pairs={{0,1},{1,0},{2,3},{3,2},{4,5},{5,4},{6,7},{7,6},{8,9},{9,8},{10,11... | collective-permute-start | bytes 393224 | tf_op jit(solution)/shard_map/ppermute | solution.py:552
  28.3 10.8 %collective-permute-start.5 = (f32[16,2048]{1,0:T(8,128)S(1)}, f32[16,2048]{1,0:T(8,128)S(1)}, u32[]{:S(2)}, u32[]{:S(2)}) collective-permute-start(f32[16,2048]{1,0:T(8,128)S(1)} %low_kernel.1.half_low_ref), channel_id=1, source_target_pairs={{0,3},{1,2},{2,1},{3,0},{4,7},{5,6},{6,5},{7,4},{8,11},{9,10},{10,... | collective-permute-start | bytes 393224 | tf_op jit(solution)/shard_map/ppermute | solution.py:552
  31.3 10.4 %collective-permute-start.6 = (f32[16,2048]{1,0:T(8,128)S(1)}, f32[16,2048]{1,0:T(8,128)S(1)}, u32[]{:S(2)}, u32[]{:S(2)}) collective-permute-start(f32[16,2048]{1,0:T(8,128)S(1)} %low_kernel.1.half_low_ref), channel_id=1, source_target_pairs={{0,1},{1,0},{2,3},{3,2},{4,5},{5,4},{6,7},{7,6},{8,9},{9,8},{10,11... | collective-permute-start | bytes 393224 | tf_op jit(solution)/shard_map/ppermute | solution.py:552
